TPU v7x, 128 devices: a whole 4x4x4 slice. The times are simulated.
128 devices in a mesh: shard: 16 (over y_lo, x, core), ctx: 4 (over z), tp: 2 (over y_hi).
Axes of the slice: x: 4, y: 4 (y_hi: 2, y_lo: 2; y = y_hi * 2 + y_lo), z: 4, core: 2. Of those that a mesh axis runs over, the one named last changes fastest.
Arguments:
- tokens: bfloat16 [12288, 2048], P(('shard', 'ctx')), may hold values from -6 to 6
- parents: int32 [16, 16], P('shard'), may hold values from -1 to 14, as said below
- gain_attn: bfloat16 [2048], P('shard'), may hold values from 0.5 to 1.5
- w_query: bfloat16 [2048, 2048], P('shard', 'tp'), may hold values from -0.125 to 0.125
- key_weight: bfloat16 [2048, 1024], P('shard', 'tp'), may hold values from -0.125 to 0.125
- value_weight: bfloat16 [2048, 1024], P('shard', 'tp'), may hold values from -0.125 to 0.125
- w_out: bfloat16 [2048, 2048], P('tp', 'shard'), may hold values from -0.5 to 0.5
- gain_ffn: bfloat16 [2048], P('shard'), may hold values from 0.5 to 1.5
- w_gate: bfloat16 [2048, 8192], P('shard', 'tp'), may hold values from -0.125 to 0.125
- w_up: bfloat16 [2048, 8192], P('shard', 'tp'), may hold values from -0.125 to 0.125
- w_down: bfloat16 [8192, 2048], P('tp', 'shard'), may hold values from -0.0625 to 0.0625
- cotangent: bfloat16 [12288, 2048], P(('shard', 'ctx')), may hold values from -6 to 6
Outputs:
- output: bfloat16 [12288, 2048], P(('shard', 'ctx'))
- grad_tokens: bfloat16 [12288, 2048], P(('shard', 'ctx'))
- grad_gain_attn: float32 [2048], P('shard')
- grad_query: float32 [2048, 2048], P('shard', 'tp')
- grad_key: float32 [2048, 1024], P('shard', 'tp')
- grad_value: float32 [2048, 1024], P('shard', 'tp')
- grad_out: float32 [2048, 2048], P('tp', 'shard')
- grad_gain_ffn: float32 [2048], P('shard')
- grad_gate: float32 [2048, 8192], P('shard', 'tp')
- grad_up: float32 [2048, 8192], P('shard', 'tp')
- grad_down: float32 [8192, 2048], P('tp', 'shard')
Inputs may be any that keep to these rules, and one draw needn't show every extreme that they name: parents[t, 0] = -1. For s >= 1, parents[t, s] lies in [b, s - 1], where b = -1 if s < 4, else 4 * (s // 4 - 1); -1 marks a root. parents[t, 15] = 14 in every tree.
All inputs are finite; a program needn't handle non-finite values.
Results may differ from a plain program's by a relative error of at most 0.025.
Values may be sent and summed in bfloat16 or wider, within the bound.
A program may use at most 256 MiB of HBM per device.

v0:
```python
import math

import jax
import jax.numpy as jnp
from jax import lax
from jax.sharding import PartitionSpec as P

HEAD_SIZE = 256
SEG = 48
SEGS_DEV = 4


EPSILON = 1e-06
THETA = 1000042.0
NEGATIVE = -1e30
HIGHEST = lax.Precision.HIGHEST


def contract(left, right, left_axis, right_axis):
    return lax.dot_general(
        left, right, (((left_axis,), (right_axis,)), ((), ())), preferred_element_type=jnp.float32
    )


def norm_forward(value_rows, weights):
    factor = lax.rsqrt(jnp.mean(value_rows * value_rows, -1, keepdims=True) + EPSILON)
    return (value_rows * factor * weights, factor)


def norm_backward(value_rows, factor, weights, upstream):
    weighted = upstream * weights
    inner = jnp.mean(weighted * value_rows, -1, keepdims=True)
    return (
        factor * weighted - value_rows * (factor * factor * factor) * inner,
        jnp.sum(upstream * value_rows * factor, 0),
    )


def rotate(value_rows, cosine, sine):
    middle = value_rows.shape[-1] // 2
    first = value_rows[..., :middle]
    second = value_rows[..., middle:]
    return jnp.concatenate([first * cosine - second * sine, second * cosine + first * sine], -1)


def ancestry(parent_row):
    count = parent_row.shape[0]
    index = jnp.arange(count)
    links = (parent_row[:, None] == index[None, :]).astype(jnp.float32)
    identity = jnp.eye(count, dtype=jnp.float32)

    def extend(sweep, reached):
        return jnp.maximum(identity, jnp.dot(links, reached, precision=HIGHEST))

    return lax.fori_loop(0, count, extend, identity)


def scores_of(query_rows, all_keys, allowed_mask):
    raw = jnp.einsum("tgrd,kgd->grtk", query_rows, all_keys, preferred_element_type=jnp.float32)
    return jnp.where(allowed_mask, raw * (1.0 / math.sqrt(HEAD_SIZE)), NEGATIVE)


def local(
    tokens,
    parents,
    gain_attn,
    w_query,
    key_weight,
    value_weight,
    w_out,
    gain_ffn,
    w_gate,
    w_up,
    w_down,
    cotangent,
):
    local_count = tokens.shape[0]
    segments = parents.shape[1]
    heads = w_query.shape[1] // HEAD_SIZE
    groups = key_weight.shape[1] // HEAD_SIZE
    sharing = heads // groups
    reached = ancestry(parents[0])
    depth = jnp.sum(reached, 1) - 1.0
    within = jnp.arange(local_count)
    query_segment = lax.axis_index("ctx") * SEGS_DEV + within // SEG
    query_offset = within % SEG
    seg_index = jnp.arange(segments)
    query_onehot = (query_segment[:, None] == seg_index[None, :]).astype(jnp.float32)
    position = jnp.dot(query_onehot, depth, precision=HIGHEST) * SEG + query_offset.astype(
        jnp.float32
    )
    half_width = HEAD_SIZE // 2
    frequency = jnp.power(THETA, -(jnp.arange(half_width, dtype=jnp.float32) * 2.0) / HEAD_SIZE)
    angles = position[:, None] * frequency[None, :]
    cosine = jnp.cos(angles)[:, None, :]
    sine = jnp.sin(angles)[:, None, :]
    key_index = jnp.arange(segments * SEG)
    key_segment = key_index // SEG
    key_offset = key_index % SEG
    key_onehot = (key_segment[:, None] == seg_index[None, :]).astype(jnp.float32)
    linked = contract(jnp.dot(query_onehot, reached, precision=HIGHEST), key_onehot, 1, 1) > 0.5
    allowed_mask = linked & (
        (query_segment[:, None] != key_segment[None, :])
        | (key_offset[None, :] <= query_offset[:, None])
    )
    gain_one, query_full, key_full, value_full, out_full = (
        lax.all_gather(gain_attn, "shard", axis=0, tiled=True),
        lax.all_gather(w_query, "shard", axis=0, tiled=True),
        lax.all_gather(key_weight, "shard", axis=0, tiled=True),
        lax.all_gather(value_weight, "shard", axis=0, tiled=True),
        lax.all_gather(w_out, "shard", axis=1, tiled=True),
    )
    inputs = tokens.astype(jnp.float32)
    gain_first = gain_one.astype(jnp.float32)
    normed_input, factor_one = norm_forward(inputs, gain_first)
    normed_input = normed_input.astype(jnp.bfloat16)
    query_lin = jnp.dot(normed_input, query_full, preferred_element_type=jnp.float32).reshape(
        local_count, heads, HEAD_SIZE
    )
    query_rows = (
        rotate(query_lin, cosine, sine)
        .astype(jnp.bfloat16)
        .reshape(local_count, groups, sharing, HEAD_SIZE)
    )
    key_lin = jnp.dot(normed_input, key_full, preferred_element_type=jnp.float32).reshape(
        local_count, groups, HEAD_SIZE
    )
    key_rows = rotate(key_lin, cosine, sine).astype(jnp.bfloat16)
    value_rows = (
        jnp.dot(normed_input, value_full, preferred_element_type=jnp.float32)
        .astype(jnp.bfloat16)
        .reshape(local_count, groups, HEAD_SIZE)
    )
    all_keys, all_values = (
        lax.all_gather(key_rows, "ctx", axis=0, tiled=True),
        lax.all_gather(value_rows, "ctx", axis=0, tiled=True),
    )
    scores = scores_of(query_rows, all_keys, allowed_mask)
    highest = jnp.max(scores, -1, keepdims=True)
    log_total = highest + jnp.log(jnp.sum(jnp.exp(scores - highest), -1, keepdims=True))
    probs_low = jnp.exp(scores - log_total).astype(jnp.bfloat16)
    attended = jnp.einsum(
        "grtk,kgd->tgrd", probs_low, all_values, preferred_element_type=jnp.float32
    )
    attended = attended.reshape(local_count, heads * HEAD_SIZE).astype(jnp.bfloat16)
    branch = lax.psum(jnp.dot(attended, out_full, preferred_element_type=jnp.float32), "tp")
    hidden_state = inputs + branch
    gain_two, gate_full, up_full, down_full = (
        lax.all_gather(gain_ffn, "shard", axis=0, tiled=True),
        lax.all_gather(w_gate, "shard", axis=0, tiled=True),
        lax.all_gather(w_up, "shard", axis=0, tiled=True),
        lax.all_gather(w_down, "shard", axis=1, tiled=True),
    )
    gain_second = gain_two.astype(jnp.float32)
    second, factor_two = norm_forward(hidden_state, gain_second)
    second = second.astype(jnp.bfloat16)
    gating = jnp.dot(second, gate_full, preferred_element_type=jnp.float32)
    upward = jnp.dot(second, up_full, preferred_element_type=jnp.float32)
    sigmoid_gate = jax.nn.sigmoid(gating)
    swish = gating * sigmoid_gate
    inner = (swish * upward).astype(jnp.bfloat16)
    result = hidden_state + lax.psum(
        jnp.dot(inner, down_full, preferred_element_type=jnp.float32).astype(jnp.bfloat16), "tp"
    ).astype(jnp.float32)
    output = result.astype(jnp.bfloat16)
    gain_two, gate_full, up_full, down_full = (
        lax.all_gather(gain_ffn, "shard", axis=0, tiled=True),
        lax.all_gather(w_gate, "shard", axis=0, tiled=True),
        lax.all_gather(w_up, "shard", axis=0, tiled=True),
        lax.all_gather(w_down, "shard", axis=1, tiled=True),
    )
    gain_second = gain_two.astype(jnp.float32)
    d_inner = contract(cotangent, down_full, 1, 1)
    d_gating = (d_inner * upward * sigmoid_gate * (1.0 + gating * (1.0 - sigmoid_gate))).astype(
        jnp.bfloat16
    )
    d_upward = (d_inner * swish).astype(jnp.bfloat16)
    term_down = contract(cotangent, inner, 0, 0)
    term_gate = contract(second, d_gating, 0, 0)
    term_up = contract(second, d_upward, 0, 0)
    d_second = lax.psum(
        (contract(d_gating, gate_full, 1, 1) + contract(d_upward, up_full, 1, 1)).astype(
            jnp.bfloat16
        ),
        "tp",
    ).astype(jnp.float32)
    back_two, term_gain_two = norm_backward(hidden_state, factor_two, gain_second, d_second)
    d_hidden = cotangent.astype(jnp.float32) + back_two
    d_hidden_low = d_hidden.astype(jnp.bfloat16)
    gain_one, query_full, key_full, value_full, out_full = (
        lax.all_gather(gain_attn, "shard", axis=0, tiled=True),
        lax.all_gather(w_query, "shard", axis=0, tiled=True),
        lax.all_gather(key_weight, "shard", axis=0, tiled=True),
        lax.all_gather(value_weight, "shard", axis=0, tiled=True),
        lax.all_gather(w_out, "shard", axis=1, tiled=True),
    )
    gain_first = gain_one.astype(jnp.float32)
    term_out = contract(d_hidden_low, attended, 0, 0)
    d_attended = (
        contract(d_hidden_low, out_full, 1, 1)
        .astype(jnp.bfloat16)
        .reshape(local_count, groups, sharing, HEAD_SIZE)
    )
    scores = scores_of(query_rows, all_keys, allowed_mask)
    probs = jnp.exp(scores - log_total)
    probs_low = probs.astype(jnp.bfloat16)
    d_probs = jnp.einsum(
        "tgrd,kgd->grtk", d_attended, all_values, preferred_element_type=jnp.float32
    )
    d_scores = probs * (d_probs - jnp.sum(probs * d_probs, -1, keepdims=True))
    d_raw = (d_scores * (1.0 / math.sqrt(HEAD_SIZE))).astype(jnp.bfloat16)
    d_query_turned = jnp.einsum(
        "grtk,kgd->tgrd", d_raw, all_keys, preferred_element_type=jnp.float32
    ).reshape(local_count, heads, HEAD_SIZE)
    d_keys_all = jnp.einsum("grtk,tgrd->kgd", d_raw, query_rows, preferred_element_type=jnp.float32)
    d_values_all = jnp.einsum(
        "grtk,tgrd->kgd", probs_low, d_attended, preferred_element_type=jnp.float32
    )
    d_keys_turned, d_values_mine = (
        lax.psum_scatter(
            d_keys_all.astype(jnp.bfloat16), "ctx", scatter_dimension=0, tiled=True
        ).astype(jnp.float32),
        lax.psum_scatter(
            d_values_all.astype(jnp.bfloat16), "ctx", scatter_dimension=0, tiled=True
        ).astype(jnp.float32),
    )
    d_query = (
        rotate(d_query_turned, cosine, -sine)
        .astype(jnp.bfloat16)
        .reshape(local_count, heads * HEAD_SIZE)
    )
    d_keys = (
        rotate(d_keys_turned, cosine, -sine)
        .astype(jnp.bfloat16)
        .reshape(local_count, groups * HEAD_SIZE)
    )
    d_values = d_values_mine.astype(jnp.bfloat16).reshape(local_count, groups * HEAD_SIZE)
    term_query = contract(normed_input, d_query, 0, 0)
    term_key = contract(normed_input, d_keys, 0, 0)
    term_value = contract(normed_input, d_values, 0, 0)
    d_normed_part = (
        contract(d_query, query_full, 1, 1)
        + contract(d_keys, key_full, 1, 1)
        + contract(d_values, value_full, 1, 1)
    )
    d_normed = lax.psum(d_normed_part.astype(jnp.bfloat16), "tp").astype(jnp.float32)
    back_one, term_gain_one = norm_backward(inputs, factor_one, gain_first, d_normed)
    d_tokens = (d_hidden + back_one).astype(jnp.bfloat16)
    terms = (
        term_gain_one,
        term_query,
        term_key,
        term_value,
        term_out,
        term_gain_two,
        term_gate,
        term_up,
        term_down,
    )
    shares = (
        lax.psum_scatter(
            terms[0].astype(jnp.bfloat16), "shard", scatter_dimension=0, tiled=True
        ).astype(jnp.float32),
        lax.psum_scatter(
            terms[1].astype(jnp.bfloat16), "shard", scatter_dimension=0, tiled=True
        ).astype(jnp.float32),
        lax.psum_scatter(
            terms[2].astype(jnp.bfloat16), "shard", scatter_dimension=0, tiled=True
        ).astype(jnp.float32),
        lax.psum_scatter(
            terms[3].astype(jnp.bfloat16), "shard", scatter_dimension=0, tiled=True
        ).astype(jnp.float32),
        lax.psum_scatter(
            terms[4].astype(jnp.bfloat16), "shard", scatter_dimension=0, tiled=True
        ).astype(jnp.float32),
        lax.psum_scatter(
            terms[5].astype(jnp.bfloat16), "shard", scatter_dimension=0, tiled=True
        ).astype(jnp.float32),
        lax.psum_scatter(
            terms[6].astype(jnp.bfloat16), "shard", scatter_dimension=0, tiled=True
        ).astype(jnp.float32),
        lax.psum_scatter(
            terms[7].astype(jnp.bfloat16), "shard", scatter_dimension=0, tiled=True
        ).astype(jnp.float32),
        lax.psum_scatter(
            terms[8].astype(jnp.bfloat16), "shard", scatter_dimension=0, tiled=True
        ).astype(jnp.float32),
    )
    shares = (
        lax.psum(shares[0].astype(jnp.bfloat16), "ctx").astype(jnp.float32),
        lax.psum(shares[1].astype(jnp.bfloat16), "ctx").astype(jnp.float32),
        lax.psum(shares[2].astype(jnp.bfloat16), "ctx").astype(jnp.float32),
        lax.psum(shares[3].astype(jnp.bfloat16), "ctx").astype(jnp.float32),
        lax.psum(shares[4].astype(jnp.bfloat16), "ctx").astype(jnp.float32),
        lax.psum(shares[5].astype(jnp.bfloat16), "ctx").astype(jnp.float32),
        lax.psum(shares[6].astype(jnp.bfloat16), "ctx").astype(jnp.float32),
        lax.psum(shares[7].astype(jnp.bfloat16), "ctx").astype(jnp.float32),
        lax.psum(shares[8].astype(jnp.bfloat16), "ctx").astype(jnp.float32),
    )
    return (
        output,
        d_tokens,
        shares[0],
        shares[1],
        shares[2],
        shares[3],
        jnp.transpose(shares[4]),
        shares[5],
        shares[6],
        shares[7],
        jnp.transpose(shares[8]),
    )


def solution(mesh):
    placed = (
        P(("shard", "ctx"), None),
        P("shard", None),
        P("shard"),
        P("shard", "tp"),
        P("shard", "tp"),
        P("shard", "tp"),
        P("tp", "shard"),
        P("shard"),
        P("shard", "tp"),
        P("shard", "tp"),
        P("tp", "shard"),
        P(("shard", "ctx"), None),
    )
    return jax.shard_map(
        local,
        mesh=mesh,
        in_specs=placed,
        out_specs=(
            P(("shard", "ctx"), None),
            P(("shard", "ctx"), None),
            P("shard"),
            P("shard", "tp"),
            P("shard", "tp"),
            P("shard", "tp"),
            P("tp", "shard"),
            P("shard"),
            P("shard", "tp"),
            P("shard", "tp"),
            P("tp", "shard"),
        ),
        check_vma=False,
    )
```

profile of v0, /device:TPU:1, one launch (start us, length us, event | category | flops | bytes accessed | tf_op | source)
XLA Modules:
  0.0 1424.4 jit_solution(12805647308385476270)
XLA Ops:
  10.0 21.0 %all-gather = bf16[16,1,128]{2,1,0:T(2,128)(2,1)S(1)} all-gather(bf16[1,1,128]{2,1,0:T(2,128)(2,1)} %bitcast.153), channel_id=1, replica_groups=mesh['shard'=16,'ctx'=4,'tp'=2] {'shard'}, dimensions={0}, use_global_device_ids=true | all-gather | bytes 4352 | tf_op jit(solution)/shard_map/all_gather | solution.py:107
  31.1 13.8 while.11
  49.2 2.2 convolution_convert_fusion.9
  51.5 31.7 %all-gather.12.cloned.1.call-done = bf16[2048,512]{1,0:T(8,128)(2,1)} async-done(((bf16[128,512]{1,0:T(8,128)(2,1)}), bf16[2048,512]{1,0:T(8,128)(2,1)}) %all-gather.12.cloned.1.call-update) | async-done | bytes 2097168 | tf_op jit(solution)/shard_map/all_gather | solution.py:109
  83.2 2.2 fusion.79
  85.9 12.2 all_gather.44
  98.1 11.2 all_gather.46
  109.2 13.1 all-gather.14.cloned.1.call-done
  122.3 3.2 fusion.77
  129.9 38.9 %all-gather.16.cloned.1.call-done = bf16[1024,2048]{1,0:T(8,128)(2,1)} async-done(((bf16[1024,128]{1,0:T(8,128)(2,1)}), bf16[1024,2048]{1,0:T(8,128)(2,1)}) %all-gather.16.cloned.1.call-update) | async-done | bytes 4194320 | tf_op jit(solution)/shard_map/all_gather | solution.py:111
  168.8 4.3 fusion.85
  175.3 18.6 %all-gather.1 = bf16[16,1,128]{2,1,0:T(2,128)(2,1)S(1)} all-gather(bf16[1,1,128]{2,1,0:T(2,128)(2,1)S(1)} %bitcast.154), channel_id=1, replica_groups=mesh['shard'=16,'ctx'=4,'tp'=2] {'shard'}, dimensions={0}, use_global_device_ids=true | all-gather | bytes 4352 | tf_op jit(solution)/shard_map/all_gather | solution.py:149
  193.9 38.7 %all-reduce.13.cloned.1.call-done = f32[192,2048]{1,0:T(8,128)} async-done(((f32[192,2048]{1,0:T(8,128)}), f32[192,2048]{1,0:T(8,128)}) %all-reduce.13.cloned.1.call-update) | async-done | bytes 1572880 | tf_op jit(solution)/shard_map/psum | solution.py:146
  232.6 1.7 multiply_reduce_fusion
  235.1 90.6 %all-gather.18.cloned.1.call-done = bf16[2048,4096]{1,0:T(8,128)(2,1)} async-done(((bf16[128,4096]{1,0:T(8,128)(2,1)}), bf16[2048,4096]{1,0:T(8,128)(2,1)}) %all-gather.18.cloned.1.call-update) | async-done | bytes 16777232 | tf_op jit(solution)/shard_map/all_gather | solution.py:150
  325.7 10.8 fusion.86
  336.6 83.4 %all-gather.20.cloned.1.call-done = bf16[2048,4096]{1,0:T(8,128)(2,1)} async-done(((bf16[128,4096]{1,0:T(8,128)(2,1)}), bf16[2048,4096]{1,0:T(8,128)(2,1)}) %all-gather.20.cloned.1.call-update) | async-done | bytes 16777232 | tf_op jit(solution)/shard_map/all_gather | solution.py:151
  420.0 10.9 fusion.87
  430.9 90.7 %all-gather.22.cloned.1.call-done = bf16[4096,2048]{1,0:T(8,128)(2,1)} async-done(((bf16[4096,128]{1,0:T(8,128)(2,1)}), bf16[4096,2048]{1,0:T(8,128)(2,1)}) %all-gather.22.cloned.1.call-update) | async-done | bytes 16777232 | tf_op jit(solution)/shard_map/all_gather | solution.py:152
  521.5 12.7 multiply_convert_fusion
  534.2 13.2 fusion.88
  547.4 10.7 fusion.8
  558.3 42.6 %all-reduce.15.cloned.1.call-done = bf16[192,2048]{1,0:T(8,128)(2,1)} async-done(((bf16[192,2048]{1,0:T(8,128)(2,1)}), bf16[192,2048]{1,0:T(8,128)(2,1)}) %all-reduce.15.cloned.1.call-update) | async-done | bytes 786448 | tf_op jit(solution)/shard_map/psum | solution.py:181
  600.9 2.3 fusion.24
  603.2 1.8 fusion.21
  605.7 2.3 convolution_convert_fusion.7
  607.9 2.0 reshape.231
  610.0 3.4 fusion.33
  613.4 3.0 copy.59
  616.5 3.1 fusion.38
  619.7 9.9 fusion.32
  629.6 12.0 convert_bitcast_fusion
  641.6 20.7 %copy.66 = bf16[2048,4096]{1,0:T(8,128)(2,1)} copy(bf16[2048,4096]{0,1:T(8,128)(2,1)} %convert_bitcast_fusion) | data formatting | bytes 33554432
  666.1 3.3 convolution_convert_fusion.4
  669.7 16.3 %reduce-scatter.11.cloned.1.call-done = bf16[192,2,256]{2,0,1:T(8,128)(2,1)} async-done(((bf16[768,2,256]{2,0,1:T(8,128)(2,1)}), bf16[192,2,256]{2,0,1:T(8,128)(2,1)}) %reduce-scatter.11.cloned.1.call-update) | async-done | bytes 196624 | tf_op jit(solution)/shard_map/reduce_scatter | solution.py:220
  688.8 2.2 convolution_convert_fusion.5
  691.0 3.3 convolution_convert_fusion.2
  694.4 9.2 fusion.36
  705.7 3.5 convolution_convert_fusion.3
  709.2 12.2 convolution_convert_fusion.1
  721.7 12.2 convolution_convert_fusion
  734.1 11.1 convolution_convert_fusion.6
  746.0 1.5 convolution_add_fusion
  747.6 1.7 fusion.9
  749.4 36.3 %reduce-scatter.25.cloned.1.call-done = bf16[128,4096]{1,0:T(8,128)(2,1)} async-done(((bf16[2048,4096]{1,0:T(8,128)(2,1)}), bf16[128,4096]{1,0:T(8,128)(2,1)}) %reduce-scatter.25.cloned.1.call-update) | async-done | bytes 1048592
  785.7 2.3 copy.67
  788.0 60.6 %reduce-scatter.17.cloned.1.call-done = bf16[128,512]{1,0:T(8,128)(2,1)} async-done(((bf16[2048,512]{1,0:T(8,128)(2,1)}), bf16[128,512]{1,0:T(8,128)(2,1)}) %reduce-scatter.17.cloned.1.call-update) | async-done | bytes 131088 | tf_op jit(solution)/shard_map/reduce_scatter | solution.py:270
  848.6 64.8 %reduce-scatter.15.cloned.1.call-done = bf16[128,512]{1,0:T(8,128)(2,1)} async-done(((bf16[2048,512]{1,0:T(8,128)(2,1)}), bf16[128,512]{1,0:T(8,128)(2,1)}) %reduce-scatter.15.cloned.1.call-update) | async-done | bytes 131088 | tf_op jit(solution)/shard_map/reduce_scatter | solution.py:267
  913.4 67.5 %reduce-scatter.19.cloned.1.call-done = bf16[128,1024]{1,0:T(8,128)(2,1)} async-done(((bf16[2048,1024]{1,0:T(8,128)(2,1)}), bf16[128,1024]{1,0:T(8,128)(2,1)}) %reduce-scatter.19.cloned.1.call-update) | async-done | bytes 262160 | tf_op jit(solution)/shard_map/reduce_scatter | solution.py:273
  980.9 67.7 %reduce-scatter.13.cloned.1.call-done = bf16[128,1024]{1,0:T(8,128)(2,1)} async-done(((bf16[2048,1024]{1,0:T(8,128)(2,1)}), bf16[128,1024]{1,0:T(8,128)(2,1)}) %reduce-scatter.13.cloned.1.call-update) | async-done | bytes 262160 | tf_op jit(solution)/shard_map/reduce_scatter | solution.py:264
  1048.6 101.4 %reduce-scatter.21.cloned.1.call-done = bf16[128,4096]{1,0:T(8,128)(2,1)} async-done(((bf16[2048,4096]{1,0:T(8,128)(2,1)}), bf16[128,4096]{1,0:T(8,128)(2,1)}) %reduce-scatter.21.cloned.1.call-update) | async-done | bytes 1048592 | tf_op jit(solution)/shard_map/reduce_scatter | solution.py:279
  1150.0 99.3 %reduce-scatter.23.cloned.1.call-done = bf16[128,4096]{1,0:T(8,128)(2,1)} async-done(((bf16[2048,4096]{1,0:T(8,128)(2,1)}), bf16[128,4096]{1,0:T(8,128)(2,1)}) %reduce-scatter.23.cloned.1.call-update) | async-done | bytes 1048592 | tf_op jit(solution)/shard_map/reduce_scatter | solution.py:282
  1250.6 61.8 %all-reduce.21.cloned.1.call-done = (bf16[192,2048]{1,0:T(8,128)(2,1)}, bf16[192,2048]{1,0:T(8,128)(2,1)}) async-done(((bf16[192,2048]{1,0:T(8,128)(2,1)}, bf16[192,2048]{1,0:T(8,128)(2,1)}), (bf16[192,2048]{1,0:T(8,128)(2,1)}, bf16[192,2048]{1,0:T(8,128)(2,1)})) %all-reduce.21.cloned.1.call-update) | async-done | bytes 1572880 | tf_op jit(solution)/shard_map/psum | solution.py:162
  1312.4 1.9 fusion.31
  1314.3 27.7 %all-reduce.3 = (bf16[2048]{0:T(1024)(128)(2,1)S(1)}, bf16[2048]{0:T(1024)(128)(2,1)S(1)}) all-reduce(bf16[2048]{0:T(1024)(128)(2,1)S(1)} %get-tuple-element.79, bf16[2048]{0:T(1024)(128)(2,1)S(1)} %copy-done.34), channel_id=4, replica_groups=mesh['shard'=16,'ctx'=4,'tp'=2] {'shard'}, use_global_device_ids=true, to_apply=%region_17.18.clone | all-reduce | flops 4096 | bytes 16384
  1342.1 9.9 all-reduce.4
  1353.1 2.2 add_convert_fusion
  1356.7 48.8 %all-reduce.19.cloned.1.call-done = (bf16[1024,128]{0,1:T(8,128)(2,1)}, bf16[128,1024]{1,0:T(8,128)(2,1)}, bf16[128,512]{1,0:T(8,128)(2,1)}, bf16[128,512]{1,0:T...) async-done(((bf16[1024,128]{0,1:T(8,128)(2,1)}, bf16[128,1024]{1,0:T(8,128)(2,1)}, bf16[128,512]{1,0:T(8,128)(2,1)}, ...) | async-done | bytes 3932176 | tf_op jit(solution)/shard_map/psum | solution.py:294
  1405.5 1.9 convert_element_type.230
  1407.4 1.6 convert_element_type.232
  1409.0 1.7 convert_element_type.234
  1410.7 1.9 copy.60
  1412.6 1.5 convert_element_type.239
  1414.2 1.5 convert_element_type.241
  (205 shorter events, 43.8 us)
Async XLA Ops:
  7.2 42.0 %copy-start = (bf16[192,2048]{1,0:T(8,128)(2,1)S(1)}, bf16[192,2048]{1,0:T(8,128)(2,1)}, u32[]{:S(2)}) copy-start(bf16[192,2048]{1,0:T(8,128)(2,1)} %param.14) | copy-start | bytes 2359300
  7.2 42.0 %all-gather.10.cloned.1.call-start = ((), (), s32[]{:S(2)}) async-start(), calls=%async_computation.8 | async-start | bytes 2228224 | tf_op jit(solution)/shard_map/all_gather | solution.py:110
  7.9 75.2 %all-gather.12.cloned.1.call-start = ((), (), s32[]{:S(2)}) async-start(), calls=%async_computation.9 | async-start | bytes 2228224 | tf_op jit(solution)/shard_map/all_gather | solution.py:109
  8.7 113.6 %all-gather.14.cloned.1.call-start = ((), (), s32[]{:S(2)}) async-start(), calls=%async_computation.10 | async-start | bytes 4456448 | tf_op jit(solution)/shard_map/all_gather | solution.py:108
  9.4 159.4 %all-gather.16.cloned.1.call-start = ((), (), s32[]{:S(2)}) async-start(), calls=%async_computation.11 | async-start | bytes 4456448 | tf_op jit(solution)/shard_map/all_gather | solution.py:111
  10.0 222.6 %all-reduce.13.cloned.1.call-start = ((), (), s32[]{:S(2)}) async-start(), calls=%async_computation.12 | async-start | bytes 3145728 | tf_op jit(solution)/shard_map/psum | solution.py:146
  47.4 74.9 %copy-start.30 = (f32[192]{0:T(256)}, f32[192]{0:T(256)S(1)}, u32[]{:S(2)}) copy-start(f32[192]{0:T(256)S(1)} %get-tuple-element.121) | copy-start | bytes 2308
  49.2 76.7 %copy-start.12 = (f32[192,128]{1,0:T(8,128)}, f32[192,128]{1,0:T(8,128)S(1)}, u32[]{:S(2)}) copy-start(f32[192,128]{1,0:T(8,128)S(1)} %get-tuple-element.119) | copy-start | bytes 294916
  98.1 30.5 %copy-start.7 = (bf16[768,2,256]{2,0,1:T(8,128)(2,1)}, bf16[768,2,256]{2,0,1:T(8,128)(2,1)S(1)}, u32[]{:S(2)}) copy-start(bf16[768,2,256]{2,0,1:T(8,128)(2,1)S(1)} %all_gather.44) | copy-start | bytes 2359300
  125.9 1.1 copy-start.23
  126.1 1.6 copy-start.26
  126.2 1.5 copy-start.27
  127.7 1.5 copy-start.4
  128.5 1.1 copy-start.28
  173.1 2.2 copy-start.37
  173.1 152.6 %all-gather.18.cloned.1.call-start = ((), (), s32[]{:S(2)}) async-start(), calls=%async_computation.13 | async-start | bytes 17825792 | tf_op jit(solution)/shard_map/all_gather | solution.py:150
  173.7 246.3 %all-gather.20.cloned.1.call-start = ((), (), s32[]{:S(2)}) async-start(), calls=%async_computation.14 | async-start | bytes 17825792 | tf_op jit(solution)/shard_map/all_gather | solution.py:151
  174.5 347.1 %all-gather.22.cloned.1.call-start = ((), (), s32[]{:S(2)}) async-start(), calls=%async_computation.15 | async-start | bytes 17825792 | tf_op jit(solution)/shard_map/all_gather | solution.py:152
  175.2 425.7 %all-reduce.15.cloned.1.call-start = ((), (), s32[]{:S(2)}) async-start(), calls=%async_computation.16 | async-start | bytes 1572864 | tf_op jit(solution)/shard_map/psum | solution.py:181
  234.9 90.9 %copy-start.32 = (f32[192]{0:T(256)}, f32[192]{0:T(256)S(1)}, u32[]{:S(2)}) copy-start(f32[192]{0:T(256)S(1)} %get-tuple-element.123) | copy-start | bytes 2308
  235.1 184.9 %copy-start.6 = (bf16[192,2048]{1,0:T(8,128)(2,1)}, bf16[192,2048]{1,0:T(8,128)(2,1)S(1)}, u32[]{:S(2)}) copy-start(bf16[192,2048]{1,0:T(8,128)(2,1)S(1)} %multiply_convert_fusion.3) | copy-start | bytes 2359300
  336.6 185.0 %copy-start.9 = (bf16[192,2048]{1,0:T(8,128)(2,1)S(1)}, bf16[192,2048]{1,0:T(8,128)(2,1)}, u32[]{:S(2)}) copy-start(bf16[192,2048]{1,0:T(8,128)(2,1)} %param.25) | copy-start | bytes 2359300
  534.2 13.2 copy-start.16
  558.1 106.2 %all-reduce.17.cloned.1.call-start = ((), (), s32[]{:S(2)}) async-start(), calls=%async_computation.25 | async-start | bytes 1572864
  600.9 2.3 copy-start.10
  600.9 2.3 copy-start.33
  600.9 2.3 copy-start.35
  603.2 2.4 copy-start.5
  605.7 4.3 copy-start.29
  616.5 69.5 %reduce-scatter.11.cloned.1.call-start = ((), (), s32[]{:S(2)}) async-start(), calls=%async_computation.17 | async-start | bytes 983040 | tf_op jit(solution)/shard_map/reduce_scatter | solution.py:220
  629.6 156.1 %reduce-scatter.25.cloned.1.call-start = ((), (), s32[]{:S(2)}) async-start(), calls=%async_computation.24 | async-start | bytes 17825792
  662.3 3.8 copy-start.31
  662.3 186.3 %reduce-scatter.17.cloned.1.call-start = ((), (), s32[]{:S(2)}) async-start(), calls=%async_computation.20 | async-start | bytes 2228224 | tf_op jit(solution)/shard_map/reduce_scatter | solution.py:270
  665.4 0.7 copy-start.21
  669.4 243.9 %reduce-scatter.15.cloned.1.call-start = ((), (), s32[]{:S(2)}) async-start(), calls=%async_computation.19 | async-start | bytes 2228224 | tf_op jit(solution)/shard_map/reduce_scatter | solution.py:267
  686.0 2.8 copy-start.1
  688.1 0.7 copy-start.24
  691.0 290.0 %reduce-scatter.19.cloned.1.call-start = ((), (), s32[]{:S(2)}) async-start(), calls=%async_computation.21 | async-start | bytes 4456448 | tf_op jit(solution)/shard_map/reduce_scatter | solution.py:273
  694.3 10.5 copy-start.13
  694.3 10.5 copy-start.20
  694.3 354.3 %reduce-scatter.13.cloned.1.call-start = ((), (), s32[]{:S(2)}) async-start(), calls=%async_computation.18 | async-start | bytes 4456448 | tf_op jit(solution)/shard_map/reduce_scatter | solution.py:264
  703.5 2.1 copy-start.2
  709.2 440.9 %reduce-scatter.21.cloned.1.call-start = ((), (), s32[]{:S(2)}) async-start(), calls=%async_computation.22 | async-start | bytes 17825792 | tf_op jit(solution)/shard_map/reduce_scatter | solution.py:279
  721.4 527.9 %reduce-scatter.23.cloned.1.call-start = ((), (), s32[]{:S(2)}) async-start(), calls=%async_computation.23 | async-start | bytes 17825792 | tf_op jit(solution)/shard_map/reduce_scatter | solution.py:282
  734.0 578.4 %all-reduce.21.cloned.1.call-start = ((), (), s32[]{:S(2)}) async-start(), calls=%async_computation.27 | async-start | bytes 3145728 | tf_op jit(solution)/shard_map/psum | solution.py:162
  734.0 11.1 copy-start.15
  734.0 11.1 copy-start.25
  734.0 11.9 copy-start.8
  746.0 1.6 copy-start.14
  746.0 1.6 copy-start.22
  749.3 656.1 %all-reduce.19.cloned.1.call-start = ((), (), s32[]{:S(2)}) async-start(), calls=%async_computation.26 | async-start | bytes 7864320 | tf_op jit(solution)/shard_map/psum | solution.py:294
  788.0 461.4 %copy-start.38 = (u32[128]{0:T(128)S(1)}, u32[128]{0:T(128)}, u32[]{:S(2)}) copy-start(u32[128]{0:T(128)} %constant.83) | copy-start | bytes 1540
  1249.3 64.9 %copy-start.34 = (bf16[2048]{0:T(1024)(128)(2,1)S(1)}, bf16[2048]{0:T(1024)(128)(2,1)}, u32[]{:S(2)}) copy-start(bf16[2048]{0:T(1024)(128)(2,1)} %get-tuple-element.77) | copy-start | bytes 12292
  1312.4 42.9 %copy-start.36 = (f32[192]{0:T(256)S(1)}, f32[192]{0:T(256)}, u32[]{:S(2)}) copy-start(f32[192]{0:T(256)} %get-tuple-element.120) | copy-start | bytes 2308
  1352.1 3.2 copy-start.3
  1352.1 3.2 copy-start.11
  1405.5 7.1 copy-start.19
  1409.0 5.1 copy-start.18
  1414.1 1.5 copy-start.17
Sparse Core Ops, SparseCore 0:
  9.7 37.5 all-gather.9
  49.1 34.0 all-gather.11
  84.9 37.3 all-gather.13
  123.7 44.9 all-gather.15
  173.3 59.3 all-reduce.12
  234.3 91.4 all-gather.17
  327.6 92.3 all-gather.19
  421.7 99.8 all-gather.21
  558.2 42.6 all-reduce.14
  616.6 42.3 all-reduce.16
  662.0 23.9 reduce-scatter.10
  688.2 97.4 reduce-scatter.24
  788.7 59.8 reduce-scatter.16
  851.4 61.9 reduce-scatter.14
  915.6 65.2 reduce-scatter.18
  983.2 65.3 reduce-scatter.12
  1050.8 99.1 reduce-scatter.20
  1152.3 96.9 reduce-scatter.22
  1252.4 59.9 all-reduce.20
  1316.0 89.4 all-reduce.18
where the time goes:
time: 1430 us; the launch traced here: 1420 us
  waiting for transfers between devices  1060 us (74%)
  matrix products  178 us (12%)
  blocking collectives  101 us (7%)
  local copies, waits for them, and re-layouts  38.9 us (3%)
  other arithmetic  30 us (2%)
  between operations  16.6 us (1%)
    reduce_scatter x1, waiting for transfers between devices, local(): lax.psum_scatter(terms[6].astype(jnp.bfloat16), 'shard', scatter_dimensio...  101 us
    reduce_scatter x1, waiting for transfers between devices, local(): lax.psum_scatter(terms[7].astype(jnp.bfloat16), 'shard', scatter_dimensio...  99.3 us
    dot_general x15, matrix products, contract(): lax.dot_general(left, right, (((left_axis,), (right_axis,)), ((), ())), p...  92 us
    all_gather x1, waiting for transfers between devices, local(): lax.all_gather(w_down, 'shard', axis=1, tiled=True)  90.7 us
    all_gather x1, waiting for transfers between devices, local(): lax.all_gather(w_gate, 'shard', axis=0, tiled=True)  90.6 us
    all_gather x1, waiting for transfers between devices, local(): lax.all_gather(w_up, 'shard', axis=0, tiled=True)  83.4 us
    reduce_scatter x1, waiting for transfers between devices, local(): lax.psum_scatter(terms[1].astype(jnp.bfloat16), 'shard', scatter_dimensio...  67.7 us
    reduce_scatter x1, waiting for transfers between devices, local(): lax.psum_scatter(terms[4].astype(jnp.bfloat16), 'shard', scatter_dimensio...  67.5 us
  transfers between devices with their start and end apart: 20, of which 18 were waited for; matrix products, arithmetic and copies ran while one was open for 12% of the time, Pallas kernels for 0%

commit v1 on v0

v1 whole, which is shorter than its diff:
```python
import math

import jax
import jax.numpy as jnp
from jax import lax
from jax.sharding import PartitionSpec as P

HEAD = 256
SEG = 48
SEGS_DEV = 4
NSEG = 16
ROWS = 192
TREE = 768
WIDTH = 2048
FFD = 1024

EPSILON = 1e-06
THETA = 1000042.0
NEGATIVE = -1e30
HIGHEST = lax.Precision.HIGHEST
F32 = jnp.float32
BF16 = jnp.bfloat16


def contract(left, right, left_axis, right_axis):
    return lax.dot_general(
        left, right, (((left_axis,), (right_axis,)), ((), ())), preferred_element_type=F32
    )


def norm_factor(rows):
    return lax.rsqrt(jnp.mean(rows * rows, -1, keepdims=True) + EPSILON)


def norm_backward(rows, factor, weights, upstream):
    weighted = upstream * weights
    inner = jnp.mean(weighted * rows, -1, keepdims=True)
    return (
        factor * weighted - rows * (factor * factor * factor) * inner,
        jnp.sum(upstream * rows * factor, 0),
    )


def rotate(rows, cosine, sine):
    first = rows[:, : HEAD // 2]
    second = rows[:, HEAD // 2 :]
    return jnp.concatenate([first * cosine - second * sine, second * cosine + first * sine], -1)


def tables(parent_row):
    index = jnp.arange(NSEG)
    links = (parent_row[:, None] == index[None, :]).astype(F32)
    reached = links + jnp.eye(NSEG, dtype=F32)
    for _ in range(4):
        reached = jnp.minimum(jnp.dot(reached, reached, precision=HIGHEST), 1.0)
    depth = jnp.sum(reached, 1) - 1.0
    token = jnp.arange(TREE)
    segment = token // SEG
    offset = token % SEG
    onehot = (segment[:, None] == index[None, :]).astype(F32)
    position = jnp.dot(onehot, depth, precision=HIGHEST) * SEG + offset.astype(F32)
    half = HEAD // 2
    frequency = jnp.power(THETA, -(jnp.arange(half, dtype=F32) * 2.0) / HEAD)
    angles = position[:, None] * frequency[None, :]
    linked = contract(jnp.dot(onehot, reached, precision=HIGHEST), onehot, 1, 1) > 0.5
    allowed = linked & (
        (segment[:, None] != segment[None, :]) | (offset[None, :] <= offset[:, None])
    )
    return jnp.cos(angles), jnp.sin(angles), allowed


def local(
    tokens,
    parents,
    gain_attn,
    w_query,
    key_weight,
    value_weight,
    w_out,
    gain_ffn,
    w_gate,
    w_up,
    w_down,
    cotangent,
):
    z = lax.axis_index("ctx")
    t = lax.axis_index("tp")

    def cols(w, at, size):
        return lax.dynamic_slice_in_dim(w, at, size, 1)

    def rows(w, at, size):
        return lax.dynamic_slice_in_dim(w, at, size, 0)

    gains = jnp.pad(jnp.stack([gain_attn, gain_ffn], 1), ((0, 0), (0, 126)))
    attn_mine = jnp.concatenate(
        [
            cols(w_query, z * HEAD, HEAD),
            cols(key_weight, (z // 2) * HEAD, HEAD),
            cols(value_weight, (z // 2) * HEAD, HEAD),
            rows(w_out, z * HEAD, HEAD).T,
            gains,
        ],
        1,
    )
    ffn_mine = jnp.concatenate(
        [cols(w_gate, z * FFD, FFD), cols(w_up, z * FFD, FFD), rows(w_down, z * FFD, FFD).T], 1
    )
    attn_w = lax.all_gather(attn_mine, "shard", axis=0, tiled=True)
    ffn_w = lax.all_gather(ffn_mine, "shard", axis=0, tiled=True)
    x_full = lax.all_gather(tokens, "ctx", axis=0, tiled=True)
    c_full = lax.all_gather(cotangent, "ctx", axis=0, tiled=True)
    gain_one = attn_w[:, 4 * HEAD].astype(F32)
    gain_two = attn_w[:, 4 * HEAD + 1].astype(F32)
    cosine, sine, allowed = tables(parents[0])

    x_f = x_full.astype(F32)
    n1 = (x_f * norm_factor(x_f) * gain_one).astype(BF16)
    wq, wk, wv, wo = (attn_w[:, i * HEAD : (i + 1) * HEAD] for i in range(4))
    q = rotate(contract(n1, wq, 1, 0), cosine, sine).astype(BF16)
    k = rotate(contract(n1, wk, 1, 0), cosine, sine).astype(BF16)
    v = contract(n1, wv, 1, 0).astype(BF16)
    scores = jnp.where(allowed, contract(q, k, 1, 1) * (1.0 / math.sqrt(HEAD)), NEGATIVE)
    highest = jnp.max(scores, -1, keepdims=True)
    weight = jnp.exp(scores - highest)
    p = weight / jnp.sum(weight, -1, keepdims=True)
    pl_low = p.astype(BF16)
    a = contract(pl_low, v, 1, 0).astype(BF16)
    half_rows = ROWS // 2

    def own_half(rows_):
        return lax.dynamic_slice_in_dim(rows_, t * half_rows, half_rows, 0)

    def scatter(part):
        return lax.psum_scatter(
            part.astype(BF16), ("ctx", "tp"), scatter_dimension=0, tiled=True
        ).astype(F32)

    x_own = own_half(tokens).astype(F32)
    h = x_own + scatter(contract(a, wo, 1, 1))
    r2 = norm_factor(h)
    n2_own = (h * r2 * gain_two).astype(BF16)
    n2 = lax.all_gather(n2_own, ("ctx", "tp"), axis=0, tiled=True)
    wg, wu, wd = (ffn_w[:, i * FFD : (i + 1) * FFD] for i in range(3))
    g = contract(n2, wg, 1, 0)
    u = contract(n2, wu, 1, 0)
    sg = jax.nn.sigmoid(g)
    swish = g * sg
    hid = (swish * u).astype(BF16)
    d_hid = contract(c_full, wd, 1, 0)
    dg = (d_hid * u * sg * (1.0 + g * (1.0 - sg))).astype(BF16)
    du = (d_hid * swish).astype(BF16)
    dn2 = scatter(contract(dg, wg, 1, 1) + contract(du, wu, 1, 1))
    out_own = (h + scatter(contract(hid, wd, 1, 1))).astype(BF16)
    grad_ffn = jnp.concatenate(
        [
            contract(n2, dg, 0, 0).astype(BF16),
            contract(n2, du, 0, 0).astype(BF16),
            contract(c_full, hid, 0, 0).astype(BF16),
        ],
        1,
    )
    grad_ffn = lax.psum_scatter(grad_ffn, "shard", scatter_dimension=0, tiled=True)
    back_two, term_gain_two = norm_backward(h, r2, gain_two, dn2)
    dh = own_half(cotangent).astype(F32) + back_two
    dhl = lax.all_gather(dh.astype(BF16), ("ctx", "tp"), axis=0, tiled=True)
    da = contract(dhl, wo, 1, 0).astype(BF16)
    dp = contract(da, v, 1, 1)
    ds = p * (dp - jnp.sum(p * dp, -1, keepdims=True))
    draw = (ds * (1.0 / math.sqrt(HEAD))).astype(BF16)
    dq = rotate(contract(draw, k, 1, 0), cosine, -sine).astype(BF16)
    dk = rotate(contract(draw, q, 0, 0), cosine, -sine).astype(BF16)
    dv = contract(pl_low, da, 0, 0).astype(BF16)
    dn1 = scatter(contract(dq, wq, 1, 1) + contract(dk, wk, 1, 1) + contract(dv, wv, 1, 1))
    r1_own = norm_factor(x_own)
    back_one, term_gain_one = norm_backward(x_own, r1_own, gain_one, dn1)
    dtok_own = (dh + back_one).astype(BF16)
    both = lax.all_gather(jnp.concatenate([out_own, dtok_own], 1), "tp", axis=0, tiled=True)
    gain_terms = lax.psum(
        jnp.stack([term_gain_one, term_gain_two], 1), "tp"
    )
    grad_attn = jnp.concatenate(
        [
            contract(n1, dq, 0, 0).astype(BF16),
            contract(n1, dk, 0, 0).astype(BF16),
            contract(n1, dv, 0, 0).astype(BF16),
            contract(dhl, a, 0, 0).astype(BF16),
            jnp.pad(gain_terms, ((0, 0), (0, 126))).astype(BF16),
        ],
        1,
    )
    grad_attn = lax.psum_scatter(grad_attn, "shard", scatter_dimension=0, tiled=True)
    ffn_all = lax.all_gather(grad_ffn, "ctx", axis=0)
    attn_all = lax.all_gather(grad_attn, "ctx", axis=0).astype(F32)

    def wide(parts):
        return jnp.concatenate([parts[i] for i in range(parts.shape[0])], 1).astype(F32)

    grad_query = wide(attn_all[:, :, :HEAD])
    kv = attn_all[0::2, :, HEAD : 3 * HEAD] + attn_all[1::2, :, HEAD : 3 * HEAD]
    grad_key = wide(kv[:, :, :HEAD])
    grad_value = wide(kv[:, :, HEAD:])
    grad_out = wide(attn_all[:, :, 3 * HEAD : 4 * HEAD]).T
    gain_sums = jnp.sum(attn_all[:, :, 4 * HEAD :], 0)
    grad_gate = wide(ffn_all[:, :, :FFD])
    grad_up = wide(ffn_all[:, :, FFD : 2 * FFD])
    grad_down = wide(ffn_all[:, :, 2 * FFD :]).T
    return (
        both[:, :WIDTH],
        both[:, WIDTH:],
        gain_sums[:, 0],
        grad_query,
        grad_key,
        grad_value,
        grad_out,
        gain_sums[:, 1],
        grad_gate,
        grad_up,
        grad_down,
    )


def solution(mesh):
    rows = P(("shard", "ctx"), None)
    weight = P("shard", "tp")
    turned = P("tp", "shard")
    vector = P("shard")
    return jax.shard_map(
        local,
        mesh=mesh,
        in_specs=(
            rows, P("shard", None), vector, weight, weight, weight, turned, vector,
            weight, weight, turned, rows,
        ),
        out_specs=(
            rows, rows, vector, weight, weight, weight, turned, vector, weight, weight, turned,
        ),
        check_vma=False,
    )
```

time: 1430 us -> 1060 us (0.74)
  waiting for transfers between devices: 1060 us -> 781 us
  blocking collectives: 101 us -> 6.82 us
  matrix products: 178 us -> 85.7 us
  local copies, waits for them, and re-layouts: 38.9 us -> 91.2 us
  other arithmetic: 30 us -> 53.5 us
    reduce_scatter x7 -> x4, waiting for transfers between devices: 478 us -> 284 us  [scatter(): lax.psum_scatter(part.astype(BF16), ('ctx', 'tp'), scatter_dimension=0, t...]
    psum x4 -> x0, waiting for transfers between devices: 192 us -> none  [the longest x1 61.8 us: local(): lax.psum(jnp.dot(inner, down_full, preferred_element_type=jnp.float32).as...]
    dot_general x31 -> x6, matrix products: 85.9 us -> 2.23 us  [the longest x4 1.43 us: tables(): reached = jnp.minimum(jnp.dot(reached, reached, precision=HIGHEST), 1.0)]
    all_gather x4 -> x0, blocking collectives: 63 us -> none  [the longest x1 21 us: local(): lax.all_gather(gain_attn, 'shard', axis=0, tiled=True)]
    unnamed x22 -> x17, waiting for transfers between devices: 41 us -> 95.6 us
    all_gather x7 -> x9, waiting for transfers between devices: 348 us -> 401 us  [the longest x1 80.1 us: local(): ffn_w = lax.all_gather(ffn_mine, 'shard', axis=0, tiled=True)]
    unnamed x1 -> x0, blocking collectives: 27.7 us -> none
    concatenate x2 -> x7, other arithmetic: 0.23 us -> 26.3 us  [the longest x1 21.4 us: local(): jnp.concatenate([contract(n2, dg, 0, 0).astype(BF16), contract(n2, du, 0,...]
  transfers between devices with their start and end apart: 20 -> 15, of which waited for: 18 -> 15; matrix products, arithmetic and copies ran while one was open for 12% -> 12% of each run, Pallas kernels for 0% -> 0%
where the time goes in v1:
time: 1060 us; the launch traced here: 1050 us
  waiting for transfers between devices  781 us (74%)
  local copies, waits for them, and re-layouts  91.2 us (9%)
  matrix products  85.7 us (8%)
  other arithmetic  53.5 us (5%)
  between operations  15.2 us (1%)
  starting transfers between devices  11.1 us (1%)
    reduce_scatter x4, waiting for transfers between devices, scatter(): lax.psum_scatter(part.astype(BF16), ('ctx', 'tp'), scatter_dimension=0, t...  284 us
    unnamed x17, waiting for transfers between devices  95.6 us
    dot_general x27, matrix products, contract(): lax.dot_general(left, right, (((left_axis,), (right_axis,)), ((), ())), p...  83.5 us
    all_gather x1, waiting for transfers between devices, local(): ffn_w = lax.all_gather(ffn_mine, 'shard', axis=0, tiled=True)  80.1 us
    all_gather x1, waiting for transfers between devices, local(): dhl = lax.all_gather(dh.astype(BF16), ('ctx', 'tp'), axis=0, tiled=True)  61.8 us
    all_gather x1, waiting for transfers between devices, local(): n2 = lax.all_gather(n2_own, ('ctx', 'tp'), axis=0, tiled=True)  59.1 us
    unnamed x133, local copies, waits for them, and re-layouts  55.1 us
    all_gather x1, waiting for transfers between devices, local(): attn_w = lax.all_gather(attn_mine, 'shard', axis=0, tiled=True)  47.5 us
  transfers between devices with their start and end apart: 15, of which 15 were waited for; matrix products, arithmetic and copies ran while one was open for 12% of the time, Pallas kernels for 0%

profile of v1, /device:TPU:1, one launch (start us, length us, event | category | flops | bytes accessed | tf_op | source)
XLA Modules:
  0.0 1048.0 jit_solution(14503091672309192833)
XLA Ops:
  15.3 37.4 %all-gather.12.cloned.1.call-done = bf16[768,2048]{1,0:T(8,128)(2,1)} async-done(((bf16[192,2048]{1,0:T(8,128)(2,1)}), bf16[768,2048]{1,0:T(8,128)(2,1)}) %all-gather.12.cloned.1.call-update) | async-done | bytes 3145744 | tf_op jit(solution)/shard_map/all_gather | solution.py:111
  52.7 2.6 fusion
  55.3 47.5 %all-gather.14.cloned.1.call-done = bf16[2048,1152]{0,1:T(8,128)(2,1)} async-done(((bf16[128,1152]{0,1:T(8,128)(2,1)}), bf16[2048,1152]{0,1:T(8,128)(2,1)}) %all-gather.14.cloned.1.call-update) | async-done | bytes 4718608 | tf_op jit(solution)/shard_map/all_gather | solution.py:109
  103.6 2.8 fusion.2
  108.9 1.7 fusion.87
  110.7 2.2 fusion.137
  113.0 1.9 fusion.38
  114.9 3.7 online-softmax
  118.6 4.1 convolution_convert_fusion.2
  122.8 77.8 %reduce-scatter.11.cloned.1.call-done = bf16[96,2048]{1,0:T(8,128)(2,1)} async-done(((bf16[768,2048]{1,0:T(8,128)(2,1)}), bf16[96,2048]{1,0:T(8,128)(2,1)}) %reduce-scatter.11.cloned.1.call-update) | async-done | bytes 393232 | tf_op jit(solution)/shard_map/reduce_scatter | solution.py:135
  201.8 1.9 multiply_convert_fusion.2
  207.1 59.1 %all-gather.16.cloned.1.call-done = bf16[768,2048]{1,0:T(8,128)(2,1)} async-done(((bf16[96,2048]{1,0:T(8,128)(2,1)}), bf16[768,2048]{1,0:T(8,128)(2,1)}) %all-gather.16.cloned.1.call-update) | async-done | bytes 3145744 | tf_op jit(solution)/shard_map/all_gather | solution.py:143
  266.2 80.1 %all-gather.18.cloned.1.call-done = bf16[2048,3072]{0,1:T(8,128)(2,1)} async-done(((bf16[128,3072]{0,1:T(8,128)(2,1)}), bf16[2048,3072]{0,1:T(8,128)(2,1)}) %all-gather.18.cloned.1.call-update) | async-done | bytes 12582928 | tf_op jit(solution)/shard_map/all_gather | solution.py:110
  346.3 8.4 fusion.13
  354.6 32.8 %all-gather.20.cloned.1.call-done = bf16[768,2048]{1,0:T(8,128)(2,1)} async-done(((bf16[192,2048]{1,0:T(8,128)(2,1)}), bf16[768,2048]{1,0:T(8,128)(2,1)}) %all-gather.20.cloned.1.call-update) | async-done | bytes 3145744 | tf_op jit(solution)/shard_map/all_gather | solution.py:112
  387.4 6.3 fusion.3
  395.9 6.0 multiply_convert_fusion
  401.9 5.4 fusion.7
  407.3 4.9 add_convert_fusion.1
  412.3 1.3 copy-done.48
  413.6 7.0 fusion.15
  420.6 9.8 all-gather.22.cloned.1.call-start
  430.4 60.3 %reduce-scatter.15.cloned.1.call-done = bf16[96,2048]{1,0:T(8,128)(2,1)} async-done(((bf16[768,2048]{1,0:T(8,128)(2,1)}), bf16[96,2048]{1,0:T(8,128)(2,1)}) %reduce-scatter.15.cloned.1.call-update) | async-done | bytes 393232 | tf_op jit(solution)/shard_map/reduce_scatter | solution.py:135
  490.7 1.5 fusion.55
  492.2 80.5 %reduce-scatter.13.cloned.1.call-done = bf16[96,2048]{1,0:T(8,128)(2,1)} async-done(((bf16[768,2048]{1,0:T(8,128)(2,1)}), bf16[96,2048]{1,0:T(8,128)(2,1)}) %reduce-scatter.13.cloned.1.call-update) | async-done | bytes 393232 | tf_op jit(solution)/shard_map/reduce_scatter | solution.py:135
  572.8 2.6 add_convert_fusion.2
  576.2 61.8 %all-gather.22.cloned.1.call-done = bf16[768,2048]{1,0:T(8,128)(2,1)} async-done(((bf16[96,2048]{1,0:T(8,128)(2,1)}), bf16[768,2048]{1,0:T(8,128)(2,1)}) %all-gather.22.cloned.1.call-update) | async-done | bytes 3145744 | tf_op jit(solution)/shard_map/all_gather | solution.py:166
  638.0 3.3 convolution_convert_fusion.8
  645.3 1.8 fusion.83
  649.1 2.7 add_convert_fusion
  651.9 4.1 fusion.26
  656.0 2.0 fusion.25
  658.0 2.0 fusion.28
  660.6 2.0 fusion.27
  662.6 65.8 %reduce-scatter.17.cloned.1.call-done = bf16[96,2048]{1,0:T(8,128)(2,1)} async-done(((bf16[768,2048]{1,0:T(8,128)(2,1)}), bf16[96,2048]{1,0:T(8,128)(2,1)}) %reduce-scatter.17.cloned.1.call-update) | async-done | bytes 393232 | tf_op jit(solution)/shard_map/reduce_scatter | solution.py:135
  729.7 6.8 psum.7
  737.4 6.8 copy.91
  744.5 6.0 convert_bitcast_fusion
  750.5 3.9 convolution_convert_fusion
  754.4 3.9 convolution_convert_fusion.1
  758.3 21.4 %pad_maximum_fusion = bf16[2048,3072]{0,1:T(8,128)(2,1)} fusion(bf16[2048,1024]{0,1:T(8,128)(2,1)S(1)} %convert_bitcast_fusion, bf16[2048,1024]{0,1:T(8,128)(2,1)S(1)} %convolution_convert_fusion, bf16[2048,1024]{0,1:T(8,128)(2,1)S(1)} %convolution_convert_fusion.1), kind=kLoop, calls=%fused_computation | loop fusion | flops 37748736 | bytes 25165824 | tf_op jit(solution)/shard_map/concatenate | solution.py:155
  779.7 16.7 %copy.93 = bf16[2048,3072]{1,0:T(8,128)(2,1)} copy(bf16[2048,3072]{0,1:T(8,128)(2,1)} %pad_maximum_fusion) | data formatting | bytes 25165824
  799.6 12.5 %reduce-scatter.19.cloned.1.call-done = bf16[128,1152]{1,0:T(8,128)(2,1)} async-done(((bf16[2048,1152]{1,0:T(8,128)(2,1)}), bf16[128,1152]{1,0:T(8,128)(2,1)}) %reduce-scatter.19.cloned.1.call-update) | async-done | bytes 294928
  812.1 1.8 copy.92
  814.3 81.7 %reduce-scatter.21.cloned.1.call-done = bf16[128,3072]{1,0:T(8,128)(2,1)} async-done(((bf16[2048,3072]{1,0:T(8,128)(2,1)}), bf16[128,3072]{1,0:T(8,128)(2,1)}) %reduce-scatter.21.cloned.1.call-update) | async-done | bytes 786448
  895.9 2.3 copy.94
  898.2 33.5 %all-gather.24.cloned.1.call-done = bf16[192,4096]{1,0:T(8,128)(2,1)} async-done(((bf16[96,4096]{1,0:T(8,128)(2,1)}), bf16[192,4096]{1,0:T(8,128)(2,1)}) %all-gather.24.cloned.1.call-update) | async-done | bytes 1572880 | tf_op jit(solution)/shard_map/all_gather | solution.py:178
  931.7 2.7 fusion.135
  934.4 25.1 %all-gather.26.cloned.1.call-done = bf16[512,1152]{0,1:T(8,128)(2,1)} async-done(((bf16[128,1152]{0,1:T(8,128)(2,1)}), bf16[512,1152]{0,1:T(8,128)(2,1)}) %all-gather.26.cloned.1.call-update) | async-done | bytes 1179664 | tf_op jit(solution)/shard_map/all_gather | solution.py:194
  959.5 2.5 reshape.134
  962.0 6.5 slice.200
  968.5 1.6 slice.201
  970.2 1.5 fusion.134
  982.1 23.8 %all-gather.28.cloned.1.call-done = bf16[512,3072]{0,1:T(8,128)(2,1)} async-done(((bf16[128,3072]{0,1:T(8,128)(2,1)}), bf16[512,3072]{0,1:T(8,128)(2,1)}) %all-gather.28.cloned.1.call-update) | async-done | bytes 3145744 | tf_op jit(solution)/shard_map/all_gather | solution.py:193
  1005.9 5.5 reshape.133
  1011.4 11.5 %fusion.133 = (bf16[1,128,1024]{1,0,2:T(2,128)(2,1)S(1)}, bf16[1,128,1024]{1,0,2:T(2,128)(2,1)S(1)}, bf16[1,128,1024]{1,0,2:T(2,128)(2,1)}, bf16[1,128,1024]{1,0...) fusion(bf16[4,128,3072]{1,0,2:T(4,128)(2,1)} %reshape.133), kind=kLoop, calls=%fused_computation.225 | loop fusion | bytes 6291456 | tf_op jit(solution)/shard_map/slice | solution.py:197
  1024.1 1.9 copy.112
  1026.0 1.9 copy.111
  1027.9 1.9 copy.110
  1029.8 1.9 copy.117
  1031.7 1.9 copy.116
  1036.5 1.5 maximum_convert_fusion
  1038.1 1.5 maximum_convert_fusion.1
  1039.6 1.5 convert_bitcast_fusion.1
  (199 shorter events, 46.1 us)
Async XLA Ops:
  7.2 198.0 %copy-start = (bf16[4096,128]{1,0:T(8,128)(2,1)S(1)}, bf16[4096,128]{1,0:T(8,128)(2,1)}, u32[]{:S(2)}) copy-start(bf16[4096,128]{1,0:T(8,128)(2,1)} %param.22) | copy-start | bytes 3145732
  7.2 45.5 %all-gather.12.cloned.1.call-start = ((), (), s32[]{:S(2)}) async-start(), calls=%async_computation.6 | async-start | bytes 3932160 | tf_op jit(solution)/shard_map/all_gather | solution.py:111
  7.9 94.8 %all-gather.14.cloned.1.call-start = ((), (), s32[]{:S(2)}) async-start(), calls=%async_computation.7 | async-start | bytes 5013504 | tf_op jit(solution)/shard_map/all_gather | solution.py:109
  12.4 188.1 %reduce-scatter.11.cloned.1.call-start = ((), (), s32[]{:S(2)}) async-start(), calls=%async_computation.8 | async-start | bytes 3538944 | tf_op jit(solution)/shard_map/reduce_scatter | solution.py:135
  103.6 3.3 copy-start.6
  106.9 6.1 copy-start.9
  110.7 2.3 copy-start.22
  110.7 2.2 copy-start.24
  110.7 2.2 copy-start.26
  110.7 2.2 copy-start.28
  118.6 82.0 %copy-start.3 = (bf16[192,2048]{1,0:T(8,128)(2,1)S(1)}, bf16[192,2048]{1,0:T(8,128)(2,1)}, u32[]{:S(2)}) copy-start(bf16[192,2048]{1,0:T(8,128)(2,1)} %param.12) | copy-start | bytes 2359300
  122.7 143.5 %all-gather.16.cloned.1.call-start = ((), (), s32[]{:S(2)}) async-start(), calls=%async_computation.9 | async-start | bytes 3538944 | tf_op jit(solution)/shard_map/all_gather | solution.py:143
  203.7 142.5 %all-gather.18.cloned.1.call-start = ((), (), s32[]{:S(2)}) async-start(), calls=%async_computation.10 | async-start | bytes 13369344 | tf_op jit(solution)/shard_map/all_gather | solution.py:110
  206.2 181.2 %all-gather.20.cloned.1.call-start = ((), (), s32[]{:S(2)}) async-start(), calls=%async_computation.12 | async-start | bytes 3932160 | tf_op jit(solution)/shard_map/all_gather | solution.py:112
  206.8 283.9 %reduce-scatter.15.cloned.1.call-start = ((), (), s32[]{:S(2)}) async-start(), calls=%async_computation.13 | async-start | bytes 3538944 | tf_op jit(solution)/shard_map/reduce_scatter | solution.py:135
  387.4 6.7 copy-start.40
  387.4 7.6 copy-start.41
  387.4 8.5 copy-start.44
  401.9 5.4 copy-start.45
  412.2 1.4 copy-start.48
  412.2 160.5 %reduce-scatter.13.cloned.1.call-start = ((), (), s32[]{:S(2)}) async-start(), calls=%async_computation.11 | async-start | bytes 3538944 | tf_op jit(solution)/shard_map/reduce_scatter | solution.py:135
  420.6 70.1 %copy-start.4 = (bf16[192,2048]{1,0:T(8,128)(2,1)S(1)}, bf16[192,2048]{1,0:T(8,128)(2,1)}, u32[]{:S(2)}) copy-start(bf16[192,2048]{1,0:T(8,128)(2,1)} %param.12) | copy-start | bytes 2359300
  420.6 154.9 %copy-start.2 = (f32[768,768]{1,0:T(8,128)S(1)}, f32[768,768]{1,0:T(8,128)}, u32[]{:S(2)}) copy-start(f32[768,768]{1,0:T(8,128)} %get-tuple-element.70) | copy-start | bytes 7077892
  420.6 217.4 %all-gather.22.cloned.1.call-start = ((), (), s32[]{:S(2)}) async-start(), calls=%async_computation.14 | async-start | bytes 3538944 | tf_op jit(solution)/shard_map/all_gather | solution.py:166
  575.4 153.0 %reduce-scatter.17.cloned.1.call-start = ((), (), s32[]{:S(2)}) async-start(), calls=%async_computation.15 | async-start | bytes 3538944 | tf_op jit(solution)/shard_map/reduce_scatter | solution.py:135
  638.0 3.3 copy-start.21
  642.3 1.0 copy-start.29
  642.3 1.5 copy-start.23
  642.3 1.5 copy-start.25
  643.3 3.8 slice-start
  644.3 2.8 slice-start.1
  645.3 3.8 copy-start.38
  651.8 160.3 %reduce-scatter.19.cloned.1.call-start = ((), (), s32[]{:S(2)}) async-start(), calls=%async_computation.19 | async-start | bytes 5013504
  651.9 4.1 copy-start.10
  656.0 2.0 copy-start.39
  658.0 2.0 copy-start.11
  658.0 2.6 copy-start.43
  744.2 6.3 copy-start.47
  744.2 151.7 %reduce-scatter.21.cloned.1.call-start = ((), (), s32[]{:S(2)}) async-start(), calls=%async_computation.20 | async-start | bytes 13369344
  744.5 6.0 copy-start.42
  750.5 3.9 copy-start.46
  796.5 1.0 copy-start.5
  796.5 1.1 copy-start.7
  796.5 1.4 copy-start.8
  796.5 1.5 copy-start.13
  796.5 2.1 copy-start.12
  796.5 135.2 %all-gather.24.cloned.1.call-start = ((), (), s32[]{:S(2)}) async-start(), calls=%async_computation.16 | async-start | bytes 2359296 | tf_op jit(solution)/shard_map/all_gather | solution.py:178
  799.5 160.0 %all-gather.26.cloned.1.call-start = ((), (), s32[]{:S(2)}) async-start(), calls=%async_computation.17 | async-start | bytes 1474560 | tf_op jit(solution)/shard_map/all_gather | solution.py:194
  814.0 191.9 %all-gather.28.cloned.1.call-start = ((), (), s32[]{:S(2)}) async-start(), calls=%async_computation.18 | async-start | bytes 3932160 | tf_op jit(solution)/shard_map/all_gather | solution.py:193
  976.9 2.9 copy-start.33
  976.9 2.9 copy-start.34
  976.9 2.9 copy-start.35
  976.9 2.9 copy-start.36
  976.9 3.8 copy-start.30
  976.9 3.8 copy-start.31
  977.0 3.8 copy-start.32
  1034.5 1.2 copy-start.14
  1034.5 1.2 copy-start.15
  1035.5 1.0 copy-start.16
  1035.5 2.5 copy-start.17
  1035.5 2.5 copy-start.18
  1035.6 2.5 copy-start.19
  1035.6 2.5 copy-start.20
  1038.0 3.0 copy-start.1
  (2 other events, 1.6 us)
Sparse Core Ops, SparseCore 0:
  9.7 42.9 all-gather.11
  54.9 47.8 all-gather.13
  122.9 77.6 reduce-scatter.10
  203.8 62.3 all-gather.15
  268.2 77.9 all-gather.17
  347.8 39.5 all-gather.19
  412.3 78.2 reduce-scatter.14
  494.5 78.1 reduce-scatter.12
  575.6 62.3 all-gather.21
  652.0 76.3 reduce-scatter.16
  744.3 67.7 reduce-scatter.18
  814.4 81.5 reduce-scatter.20
  898.2 33.4 all-gather.23
  933.8 25.6 all-gather.25
  961.6 44.2 all-gather.27

commit v2 on v1

v2 whole, which is shorter than its diff:
```python
import functools
import math

import jax
import jax.numpy as jnp
from jax import lax
from jax.experimental import pallas as pl
from jax.experimental.pallas import tpu as pltpu
from jax.sharding import PartitionSpec as P

HEAD = 256
HALF = HEAD // 2
SEG = 48
NSEG = 16
ROWS = 192
TREE = 768
WIDTH = 2048
FFD = 1024
BLOCK = 128
GROWS = 32

EPSILON = 1e-06
THETA = 1000042.0
NEGATIVE = -1e30
HIGHEST = lax.Precision.HIGHEST
F32 = jnp.float32
BF16 = jnp.bfloat16
MESH = pl.DeviceIdType.MESH
ANY = pl.BlockSpec(memory_space=pl.ANY)
VM = pl.BlockSpec(memory_space=pltpu.VMEM)


def nn(left, right):
    return jnp.dot(left, right, preferred_element_type=F32)


def nt(left, right):
    return lax.dot_general(left, right, (((1,), (1,)), ((), ())), preferred_element_type=F32)


def tn(left, right):
    return lax.dot_general(left, right, (((0,), (0,)), ((), ())), preferred_element_type=F32)


def ring(value, step):
    return lax.rem(value + step, 4)


class Place:
    def __init__(self):
        shard = lax.axis_index("shard")
        self.shard = shard
        self.y = shard // 8
        self.x = lax.rem(shard // 2, 4)
        self.c = lax.rem(shard, 2)
        self.z = lax.axis_index("ctx")
        self.t = lax.axis_index("tp")

    def block(self, dy=0, dx=0, dc=0):
        y = 1 - self.y if dy else self.y
        c = 1 - self.c if dc else self.c
        return y * 8 + ring(self.x, dx) * 2 + c

    def to(self, dy=0, dx=0, dc=0, dz=0, dt=0):
        t = 1 - self.t if dt else self.t
        return (self.block(dy, dx, dc), ring(self.z, dz), t)


ALL_NEAR = ("y", "x+", "x-", "c", "z+", "z-", "t")
NEAR = {
    "y": dict(dy=1), "x+": dict(dx=1), "x-": dict(dx=3), "c": dict(dc=1),
    "z+": dict(dz=1), "z-": dict(dz=3), "t": dict(dt=1),
}


class Net:
    def __init__(self, here, send, recv, local):
        self.here, self.send, self.recv, self.local = here, send, recv, local
        self.sent, self.count, self.copies = [], 0, 0

    def greet(self, names):
        barrier = pltpu.get_barrier_semaphore()
        for name in names:
            pl.semaphore_signal(
                barrier, inc=1, device_id=self.here.to(**NEAR[name]), device_id_type=MESH
            )
        pl.semaphore_wait(barrier, len(names))

    def push(self, src, dst, name):
        index = self.count
        self.count += 1
        copy = pltpu.make_async_remote_copy(
            src_ref=src,
            dst_ref=dst,
            send_sem=self.send.at[index],
            recv_sem=self.recv.at[index],
            device_id=self.here.to(**NEAR[name]),
            device_id_type=MESH,
        )
        copy.start()
        self.sent.append(copy)
        return copy

    def copy(self, src, dst):
        index = self.copies
        self.copies += 1
        copy = pltpu.make_async_copy(src, dst, self.local.at[index])
        copy.start()
        return copy

    def drain(self):
        for copy in self.sent:
            copy.wait_send()


def near_sems(remote, local):
    return [
        pltpu.SemaphoreType.DMA((remote,)),
        pltpu.SemaphoreType.DMA((remote,)),
        pltpu.SemaphoreType.DMA((local,)),
    ]


def chunk(index):
    return pl.ds(pl.multiple_of(index * ROWS, ROWS), ROWS)


class RingGather:
    def __init__(self, net, own, full):
        self.net, self.full, self.rows = net, full, own.shape[0]
        half = self.rows // 2
        one, two = own.at[pl.ds(0, half)], own.at[pl.ds(half, half)]
        self.a1 = net.push(one, self.half(0, 0), "z+")
        self.b2 = net.push(two, self.half(0, 1), "z-")
        self.a2 = net.push(two, self.half(0, 1), "z+")
        self.b1 = net.push(one, self.half(0, 0), "z-")

    def half(self, step, part):
        half = self.rows // 2
        start = ring(self.net.here.z, step) * self.rows + part * half
        return self.full.at[pl.ds(pl.multiple_of(start, half), half)]

    def at(self, step):
        return span(ring(self.net.here.z, step), self.rows)

    def forward(self):
        self.a1.wait_recv()
        self.f1 = self.net.push(self.half(3, 0), self.half(3, 0), "z+")
        self.b2.wait_recv()
        self.f2 = self.net.push(self.half(1, 1), self.half(1, 1), "z-")

    def left(self):
        self.a2.wait_recv()

    def right(self):
        self.b1.wait_recv()

    def far(self):
        self.f1.wait_recv()
        self.f2.wait_recv()


class RingSum:
    def __init__(self, net, part, passed, plus, minus, mine, other, subs):
        self.net, self.part, self.passed = net, part, passed
        self.plus, self.minus, self.mine, self.other = plus, minus, mine, other
        width = part.shape[1] // subs
        self.cols = [
            (pl.ds(i * width, width // 2), pl.ds(i * width + width // 2, width // 2))
            for i in range(subs)
        ]
        self.subs = subs
        self.width = width
        self.e1, self.e2, self.r1, self.r2 = {}, {}, {}, {}
        self.s1, self.s2, self.t = {}, {}, {}

    def at(self, step):
        return chunk(ring(self.net.here.z, step))

    def far(self, i):
        one, two = self.cols[i]
        self.e1[i] = self.net.push(self.part.at[self.at(2), one], self.passed.at[:, one], "z+")
        self.e2[i] = self.net.push(self.part.at[self.at(2), two], self.passed.at[:, two], "z-")

    def raw(self, i):
        one, two = self.cols[i]
        self.r1[i] = self.net.push(self.part.at[self.at(1), two], self.plus.at[:, two], "z+")
        self.r2[i] = self.net.push(self.part.at[self.at(3), one], self.minus.at[:, one], "z-")

    def add(self, i):
        one, two = self.cols[i]
        part, passed = self.part, self.passed
        self.e1[i].wait_recv()
        part[self.at(1), one] = (
            part[self.at(1), one].astype(F32) + passed[:, one].astype(F32)
        ).astype(BF16)
        self.s1[i] = self.net.push(part.at[self.at(1), one], self.plus.at[:, one], "z+")
        self.e2[i].wait_recv()
        part[self.at(3), two] = (
            part[self.at(3), two].astype(F32) + passed[:, two].astype(F32)
        ).astype(BF16)
        self.s2[i] = self.net.push(part.at[self.at(3), two], self.minus.at[:, two], "z-")

    def cross(self, i):
        for copy in (self.r1[i], self.r2[i], self.s1[i], self.s2[i]):
            copy.wait_recv()
        both = pl.ds(i * self.width, self.width)
        self.mine[:, both] = (
            self.part[self.at(0), both].astype(F32)
            + self.plus[:, both].astype(F32)
            + self.minus[:, both].astype(F32)
        ).astype(BF16)
        self.t[i] = self.net.push(self.mine.at[:, both], self.other.at[:, both], "t")

    def arrive(self, i):
        self.t[i].wait_recv()


def ring_sum_scratch():
    return [pltpu.VMEM((ROWS, WIDTH), BF16) for _ in range(5)]


class ShardGather:
    def __init__(self, net, own, full, rows):
        self.net, self.own, self.full, self.rows = net, own, full, rows
        self.to_sibling = []

    def at(self, part=None, **step):
        block = self.net.here.block(**step)
        if part is None:
            return self.full.at[pl.ds(pl.multiple_of(block * self.rows, self.rows), self.rows)]
        half = self.rows // 2
        start = block * self.rows + part * half
        return self.full.at[pl.ds(pl.multiple_of(start, half), half)]

    def relay(self, name, part=None, **step):
        ref = self.at(part, **step)
        return self.net.push(ref, ref, name)

    def sibling(self, part=None, **step):
        self.to_sibling.append(self.relay("c", part, **step))

    def begin(self):
        self.y0, self.p0, self.m0, c0 = (
            self.net.push(self.own, self.at(), name) for name in ("y", "x+", "x-", "c")
        )
        self.to_sibling.append(c0)

    def across(self):
        self.y0.wait_recv()
        self.p1 = self.relay("x+", dy=1)
        self.m1 = self.relay("x-", dy=1)
        self.sibling(dy=1)

    def near(self, dy):
        plus, minus = (self.p1, self.m1) if dy else (self.p0, self.m0)
        plus.wait_recv()
        fp = self.relay("x+", 0, dy=dy, dx=3)
        self.sibling(dy=dy, dx=3)
        minus.wait_recv()
        fm = self.relay("x-", 1, dy=dy, dx=1)
        self.sibling(dy=dy, dx=1)
        if dy:
            self.fp1, self.fm1 = fp, fm
        else:
            self.fp0, self.fm0 = fp, fm

    def far(self, dy):
        plus, minus = (self.fp1, self.fm1) if dy else (self.fp0, self.fm0)
        plus.wait_recv()
        self.sibling(0, dy=dy, dx=2)
        minus.wait_recv()
        self.sibling(1, dy=dy, dx=2)

    def finish(self):
        for copy in self.to_sibling:
            copy.wait_recv()


class ShardSum:
    def __init__(self, net, source, rows, held, gift, passed, plus, minus, last):
        self.net, self.source, self.rows = net, source, rows
        self.held, self.gift, self.passed = held, gift, passed
        self.plus, self.minus, self.last = plus, minus, last
        self.gifts, self.loads = {}, {}
        for dx in (2, 1, 3, 0):
            for dy in (1, 0):
                self.gifts[dx, dy] = net.push(
                    self.block(dx, dy, 1), gift.at[2 * dx + dy], "c"
                )
                self.loads[dx, dy] = net.copy(self.block(dx, dy, 0), held.at[2 * dx + dy])
        self.e1, self.e2, self.raw, self.sums = {}, {}, {}, {}

    def block(self, dx, dy, dc):
        return self.source.at[span(self.net.here.block(dx=dx, dy=dy, dc=dc), self.rows)]

    def pair(self, dx, dy):
        slot = 2 * dx + dy
        self.gifts[dx, dy].wait_recv()
        self.loads[dx, dy].wait()
        self.held[slot] = self.held[slot] + self.gift[slot]
        half = self.rows // 2
        one, two = pl.ds(0, half), pl.ds(half, half)
        held = self.held
        if dx == 2:
            self.e1[dy] = self.net.push(held.at[slot, one], self.passed.at[dy, one], "x+")
            self.e2[dy] = self.net.push(held.at[slot, two], self.passed.at[dy, two], "x-")
        if dx == 1:
            self.raw[1, dy] = self.net.push(held.at[slot, two], self.plus.at[dy, two], "x+")
        if dx == 3:
            self.raw[3, dy] = self.net.push(held.at[slot, one], self.minus.at[dy, one], "x-")

    def pass_on(self, dy):
        half = self.rows // 2
        one, two = pl.ds(0, half), pl.ds(half, half)
        held, passed = self.held, self.passed
        self.e1[dy].wait_recv()
        slot = 2 + dy
        held[slot, one] = held[slot, one] + passed[dy, one]
        self.sums[1, dy] = self.net.push(held.at[slot, one], self.plus.at[dy, one], "x+")
        self.e2[dy].wait_recv()
        slot = 6 + dy
        held[slot, two] = held[slot, two] + passed[dy, two]
        self.sums[3, dy] = self.net.push(held.at[slot, two], self.minus.at[dy, two], "x-")

    def close(self, dy):
        for copy in (self.raw[1, dy], self.raw[3, dy], self.sums[1, dy], self.sums[3, dy]):
            copy.wait_recv()
        self.held[dy] = (
            self.held[dy].astype(F32) + self.plus[dy].astype(F32) + self.minus[dy].astype(F32)
        ).astype(BF16)
        if dy:
            self.cross = self.net.push(self.held.at[1], self.last, "y")

    def result(self):
        self.cross.wait_recv()
        return self.held[0].astype(F32) + self.last[...].astype(F32)


def shard_sum_scratch(rows, width):
    def block(*lead):
        return pltpu.VMEM((*lead, rows, width), BF16)

    return [block(8), block(8), block(2), block(2), block(2), block()]


def gain_row(gains, row):
    return jnp.concatenate(
        [gains[s * GROWS : s * GROWS + 16, :][row : row + 1].astype(F32) for s in range(16)], 1
    )


def factor_of(rows):
    return lax.rsqrt(jnp.mean(rows * rows, -1, keepdims=True) + EPSILON)


def turn(rows, cosine, sine):
    first, second = rows[:, :HALF], rows[:, HALF:]
    return first * cosine - second * sine, second * cosine + first * sine


def tiles(count, body):
    def step(i, carry):
        body(i)
        return carry

    lax.fori_loop(0, count, step, 0)


def span(index, size):
    return pl.ds(pl.multiple_of(index * size, size), size)


def kernel_a(
    tok, cot, ablk, fblk, gblk, cosine, sine, allowed,
    n1_o, q_o, k_o, v_o, a_o, p_o, h_o, n2_o, aw_o, g_o, fw, cf,
    xf, n1, q, k, v, a, p, part, passed, plus, minus, mine, other, aw, gains,
    send, recv, local,
):
    here = Place()
    net = Net(here, send, recv, local)
    net.greet(ALL_NEAR)
    xs = RingGather(net, tok, xf)
    gg = ShardGather(net, gblk, gains, GROWS)
    gg.begin()
    ag = ShardGather(net, ablk, aw, BLOCK)
    ag.begin()
    saved = [
        net.copy(ablk, ag.at()),
        net.copy(gblk, gg.at()),
        net.copy(fblk, fw.at[pl.ds(pl.multiple_of(here.shard * BLOCK, BLOCK), BLOCK)]),
        net.copy(cot, cf.at[chunk(here.z)]),
    ]
    xf[xs.at(0), :] = tok[...]
    gg.across()
    ag.across()
    gg.near(0)
    gg.near(1)
    ag.near(0)
    gg.far(0)
    gg.far(1)
    xs.forward()
    ag.near(1)
    gg.finish()
    saved[0].wait()
    saved[1].wait()
    ag.far(0)
    ag.far(1)
    fg = ShardGather(net, fblk, fw, BLOCK)
    fg.begin()
    cs = RingGather(net, cot, cf)
    gain_one = gain_row(gains, 0)

    def normed(step):
        at = xs.at(step)
        rows = xf[at, :].astype(F32)
        n1[at, :] = (rows * factor_of(rows) * gain_one).astype(BF16)

    def project(step):
        at = xs.at(step)
        rows = n1[at, :]
        co, si = cosine[at, :], sine[at, :]
        for dst, i in ((q, 0), (k, 1)):
            first, second = turn(nn(rows, aw[:, i * HEAD : (i + 1) * HEAD]), co, si)
            dst[at, :HALF] = first.astype(BF16)
            dst[at, HALF:] = second.astype(BF16)
        v[at, :] = nn(rows, aw[:, 2 * HEAD : 3 * HEAD]).astype(BF16)

    normed(0)
    ag.finish()
    project(0)
    xs.left()
    normed(3)
    project(3)
    xs.right()
    normed(1)
    project(1)
    xs.far()
    normed(2)
    project(2)
    fg.across()
    out_copies = [
        net.copy(n1, n1_o), net.copy(aw, aw_o), net.copy(q, q_o), net.copy(k, k_o),
        net.copy(v, v_o), net.copy(gains, g_o),
    ]

    sums = RingSum(net, part, passed, plus, minus, mine, other, 2)

    def attend(step):
        at = sums.at(step)
        scores = jnp.where(
            allowed[at, :].astype(F32) > 0.5,
            nt(q[at, :], k[...]) * (1.0 / math.sqrt(HEAD)),
            NEGATIVE,
        )
        weight = jnp.exp(scores - jnp.max(scores, -1, keepdims=True))
        probs = weight / jnp.sum(weight, -1, keepdims=True)
        p[at, :] = probs
        a[at, :] = nn(probs.astype(BF16), v[...]).astype(BF16)

    def branch(step):
        at = sums.at(step)
        rows = a[at, :]

        def body(j):
            part[at, span(j, 512)] = nt(
                rows, aw[span(j, 512), 3 * HEAD : 4 * HEAD]
            ).astype(BF16)

        tiles(4, body)

    attend(2)
    branch(2)
    sums.far(0)
    sums.far(1)
    attend(1)
    branch(1)
    attend(3)
    branch(3)
    sums.raw(0)
    sums.raw(1)
    fg.near(0)
    sums.add(0)
    cs.forward()
    attend(0)
    branch(0)
    sums.add(1)
    out_copies += [net.copy(a, a_o), net.copy(p, p_o)]
    fg.near(1)
    sums.cross(0)
    fg.far(0)
    sums.cross(1)
    fg.far(1)
    cs.left()
    cs.right()
    cs.far()
    sums.arrive(0)
    sums.arrive(1)
    hidden = tok[...].astype(F32) + mine[...].astype(F32) + other[...].astype(F32)
    h_o[...] = hidden
    n2_o[...] = (hidden * factor_of(hidden) * gain_row(gains, 1)).astype(BF16)
    fg.finish()
    for copy in saved[2:] + out_copies:
        copy.wait()
    net.drain()


def out(shape, kind=BF16):
    return jax.ShapeDtypeStruct(shape, kind)


def params(number):
    return pltpu.CompilerParams(
        collective_id=number, has_side_effects=True, vmem_limit_bytes=60 * 1024 * 1024
    )


def call_a(tok, cot, ablk, fblk, gblk, cosine, sine, allowed):
    rows_b = pltpu.VMEM((TREE, WIDTH), BF16)
    head_b = pltpu.VMEM((TREE, HEAD), BF16)
    return pl.pallas_call(
        kernel_a,
        out_shape=[
            out((TREE, WIDTH)), out((TREE, HEAD)), out((TREE, HEAD)), out((TREE, HEAD)),
            out((TREE, HEAD)), out((TREE, TREE), F32), out((ROWS, WIDTH), F32),
            out((ROWS, WIDTH)), out((WIDTH, 4 * HEAD)), out((16 * GROWS, 128)),
            out((WIDTH, 3 * FFD)), out((TREE, WIDTH)),
        ],
        in_specs=[VM] * 8,
        out_specs=[ANY] * 6 + [VM] * 2 + [ANY] * 4,
        scratch_shapes=[
            rows_b, rows_b, head_b, head_b, head_b, head_b, pltpu.VMEM((TREE, TREE), F32), rows_b,
            *ring_sum_scratch(),
            pltpu.VMEM((WIDTH, 4 * HEAD), BF16), pltpu.VMEM((16 * GROWS, 128), BF16),
            *near_sems(96, 16),
        ],
        compiler_params=params(0),
        name="attend",
    )(tok, cot, ablk, fblk, gblk, cosine, sine, allowed)


def kernel_f(
    n2_in, h_in, fw, cf, gains,
    dh_o, low_o, out_o, grads_o, term_o,
    w, c, n2, dgu, hid,
    part, passed, plus, minus, mine, other,
    part2, passed2, plus2, minus2, mine2, other2,
    send, recv, local,
):
    here = Place()
    net = Net(here, send, recv, local)
    net.greet(("z+", "z-", "t"))
    ns = RingGather(net, n2_in, n2)
    loads = [net.copy(fw, w), net.copy(cf, c)]
    n2[ns.at(0), :] = n2_in[...]
    for copy in loads:
        copy.wait()

    def feed(step):
        at = ns.at(step)

        def body(j):
            cols = span(j, 256)
            rows = n2[at, :]
            g = nn(rows, w[:, cols])
            u = nn(rows, w[:, pl.ds(pl.multiple_of(FFD + j * 256, 256), 256)])
            d = nn(c[at, :], w[:, pl.ds(pl.multiple_of(2 * FFD + j * 256, 256), 256)])
            s = jax.nn.sigmoid(g)
            swish = g * s
            hid[at, cols] = (swish * u).astype(BF16)
            dgu[at, cols] = (d * u * s * (1.0 + g * (1.0 - s))).astype(BF16)
            dgu[at, pl.ds(pl.multiple_of(FFD + j * 256, 256), 256)] = (d * swish).astype(BF16)

        tiles(4, body)

    feed(0)
    ns.forward()
    ns.left()
    feed(3)
    ns.right()
    feed(1)
    ns.far()
    feed(2)
    sums = RingSum(net, part, passed, plus, minus, mine, other, 2)
    outs = RingSum(net, part2, passed2, plus2, minus2, mine2, other2, 2)

    def back(step):
        at = sums.at(step)

        def body(j):
            part[at, span(j, 512)] = nt(dgu[at, :], w[span(j, 512), : 2 * FFD]).astype(BF16)

        tiles(4, body)

    def down(step):
        at = sums.at(step)

        def body(j):
            part2[at, span(j, 512)] = nt(hid[at, :], w[span(j, 512), 2 * FFD :]).astype(BF16)

        tiles(4, body)

    back(2)
    sums.far(0)
    sums.far(1)
    back(1)
    back(3)
    sums.raw(0)
    sums.raw(1)
    sums.add(0)
    back(0)
    sums.add(1)
    down(2)
    outs.far(0)
    outs.far(1)
    down(1)
    down(3)
    outs.raw(0)
    outs.raw(1)
    down(0)
    sums.cross(0)

    def grad(i):
        turned = n2[:, span(i, 256)].T
        for j in range(4):
            w[span(i, 256), j * 512 : (j + 1) * 512] = nn(
                turned, dgu[:, j * 512 : (j + 1) * 512]
            ).astype(BF16)

    def grad_down(i):
        turned = c[:, span(i, 256)].T
        for j in range(2):
            w[span(i, 256), 2 * FFD + j * 512 : 2 * FFD + (j + 1) * 512] = nn(
                turned, hid[:, j * 512 : (j + 1) * 512]
            ).astype(BF16)

    tiles(4, grad)
    sums.cross(1)
    outs.add(0)
    outs.add(1)
    tiles(4, lambda i: grad(i + 4))
    tiles(8, grad_down)
    saves = [net.copy(w, grads_o)]
    sums.arrive(0)
    sums.arrive(1)
    hidden = h_in[...]
    upstream = mine[...].astype(F32) + other[...].astype(F32)
    factor = factor_of(hidden)
    weighted = upstream * gain_row(gains, 1)
    inner = jnp.mean(weighted * hidden, -1, keepdims=True)
    dh = (
        c[ns.at(0), :].astype(F32) + factor * weighted - hidden * (factor * factor * factor) * inner
    )
    dh_o[...] = dh
    low_o[...] = dh.astype(BF16)
    term_o[...] = jnp.sum(upstream * hidden * factor, 0, keepdims=True)
    outs.cross(0)
    outs.cross(1)
    outs.arrive(0)
    outs.arrive(1)
    out_o[...] = (
        h_in[...] + (mine2[...].astype(F32) + other2[...].astype(F32))
    ).astype(BF16)
    for copy in saves:
        copy.wait()
    net.drain()


def call_f(n2_in, h_in, fw, cf, gains):
    rows_b = pltpu.VMEM((TREE, WIDTH), BF16)
    return pl.pallas_call(
        kernel_f,
        out_shape=[
            out((ROWS, WIDTH), F32), out((ROWS, WIDTH)), out((ROWS, WIDTH)),
            out((WIDTH, 3 * FFD)), out((1, WIDTH), F32),
        ],
        in_specs=[VM, VM, ANY, ANY, VM],
        out_specs=[VM, VM, VM, ANY, VM],
        scratch_shapes=[
            pltpu.VMEM((WIDTH, 3 * FFD), BF16), rows_b, rows_b, rows_b,
            pltpu.VMEM((TREE, FFD), BF16),
            rows_b, *ring_sum_scratch(), rows_b, *ring_sum_scratch(),
            *near_sems(40, 8),
        ],
        compiler_params=params(1),
        name="feed",
    )(n2_in, h_in, fw, cf, gains)


def kernel_b(
    low_in, dh_in, tok, cosine, sine, gains, term_in, p_in, q_in, k_in, v_in, a_in, n1_in, aw_in, fgrads,
    dtok_o, agrads_o, terms_o, fblk_o,
    low, p, q, k, v, a, n1, aw, da, d, dk, dv,
    part, passed, plus, minus, mine, other,
    held, gift, fpassed, fplus, fminus, flast,
    send, recv, local,
):
    here = Place()
    net = Net(here, send, recv, local)
    net.greet(ALL_NEAR)
    ls = RingGather(net, low_in, low)
    loads = [
        net.copy(src, dst)
        for src, dst in (
            (aw_in, aw), (v_in, v), (p_in, p), (k_in, k), (q_in, q), (a_in, a), (n1_in, n1)
        )
    ]
    fs = ShardSum(net, fgrads, BLOCK, held, gift, fpassed, fplus, fminus, flast)
    low[ls.at(0), :] = low_in[...]

    def attended(step):
        at = ls.at(step)
        da[at, :] = nn(low[at, :], aw[:, 3 * HEAD : 4 * HEAD]).astype(BF16)

    loads[0].wait()
    attended(0)
    ls.forward()
    fs.pair(2, 1)
    fs.pair(2, 0)
    ls.left()
    attended(3)
    ls.right()
    attended(1)
    fs.pair(1, 1)
    fs.pair(3, 1)
    fs.pair(1, 0)
    fs.pair(3, 0)
    for copy in loads[1:]:
        copy.wait()
    fs.pass_on(1)
    ls.far()
    attended(2)

    def attend(step):
        at = ls.at(step)
        da_rows, probs = da[at, :], p[at, :]
        dp = nt(da_rows, v[...])
        ds = probs * (dp - jnp.sum(probs * dp, -1, keepdims=True))
        draw = (ds * (1.0 / math.sqrt(HEAD))).astype(BF16)
        first, second = turn(nn(draw, k[...]), cosine[at, :], -sine[at, :])
        d[at, :HALF] = first.astype(BF16)
        d[at, HALF:HEAD] = second.astype(BF16)
        dk_more, dv_more = tn(draw, q[at, :]), tn(probs.astype(BF16), da_rows)
        if step == 0:
            dk[...] = dk_more
            dv[...] = dv_more
        else:
            dk[...] += dk_more
            dv[...] += dv_more

    for step in range(4):
        attend(step)
    first, second = turn(dk[...], cosine[...], -sine[...])
    d[:, HEAD : HEAD + HALF] = first.astype(BF16)
    d[:, HEAD + HALF : 2 * HEAD] = second.astype(BF16)
    d[:, 2 * HEAD :] = dv[...].astype(BF16)

    sums = RingSum(net, part, passed, plus, minus, mine, other, 2)

    def back(step):
        at = sums.at(step)

        def body(j):
            part[at, span(j, 512)] = nt(d[at, :], aw[span(j, 512), : 3 * HEAD]).astype(BF16)

        tiles(4, body)

    back(2)
    sums.far(0)
    sums.far(1)
    back(1)
    back(3)
    sums.raw(0)
    sums.raw(1)
    fs.pass_on(0)
    sums.add(0)
    back(0)
    sums.add(1)

    def grad(i):
        turned = n1[:, span(i, 256)].T
        aw[span(i, 256), : 3 * HEAD] = nn(turned, d[...]).astype(BF16)
        turned = low[:, span(i, 256)].T
        aw[span(i, 256), 3 * HEAD :] = nn(turned, a[...]).astype(BF16)

    tiles(8, grad)
    saves = [net.copy(aw, agrads_o)]
    fs.pair(0, 1)
    fs.pair(0, 0)
    sums.cross(0)
    sums.cross(1)
    fs.close(1)
    fs.close(0)
    sums.arrive(0)
    sums.arrive(1)
    inputs = tok[...].astype(F32)
    upstream = mine[...].astype(F32) + other[...].astype(F32)
    factor = factor_of(inputs)
    weighted = upstream * gain_row(gains, 0)
    inner = jnp.mean(weighted * inputs, -1, keepdims=True)
    dtok_o[...] = (
        dh_in[...] + (factor * weighted - inputs * (factor * factor * factor) * inner)
    ).astype(BF16)
    term_one = jnp.sum(upstream * inputs * factor, 0, keepdims=True)
    term_two = term_in[...]
    row = lax.broadcasted_iota(jnp.int32, (GROWS, 128), 0)
    for s in range(16):
        cols = slice(s * 128, (s + 1) * 128)
        terms_o[s * GROWS : (s + 1) * GROWS, :] = jnp.where(
            row == 0, term_one[:, cols], jnp.where(row == 1, term_two[:, cols], 0.0)
        ).astype(BF16)
    fblk_o[...] = fs.result().astype(BF16)
    for copy in saves:
        copy.wait()
    net.drain()


def call_b(low, dh, tok, cosine, sine, gains, term, p, q, k, v, a, n1, aw, fgrads):
    rows_b = pltpu.VMEM((TREE, WIDTH), BF16)
    head_b = pltpu.VMEM((TREE, HEAD), BF16)
    head_f = pltpu.VMEM((TREE, HEAD), F32)
    return pl.pallas_call(
        kernel_b,
        out_shape=[
            out((ROWS, WIDTH)), out((WIDTH, 4 * HEAD)), out((16 * GROWS, 128)),
            out((BLOCK, 3 * FFD)),
        ],
        in_specs=[VM] * 7 + [ANY] * 8,
        out_specs=[VM, ANY, VM, VM],
        scratch_shapes=[
            rows_b, pltpu.VMEM((TREE, TREE), F32), head_b, head_b, head_b, head_b, rows_b,
            pltpu.VMEM((WIDTH, 4 * HEAD), BF16), head_b, pltpu.VMEM((TREE, 3 * HEAD), BF16),
            head_f, head_f,
            rows_b, *ring_sum_scratch(),
            *shard_sum_scratch(BLOCK, 3 * FFD),
            *near_sems(64, 24),
        ],
        compiler_params=params(2),
        name="attend_back",
    )(low, dh, tok, cosine, sine, gains, term, p, q, k, v, a, n1, aw, fgrads)


def kernel_r(
    agrads, terms, fblk,
    gone_o, query_o, key_o, value_o, wout_o, gtwo_o, gate_o, up_o, down_o,
    ffull, afull, gfull, ablk, gblk,
    held, gift, passed, plus, minus, last,
    gheld, ggift, gpassed, gplus, gminus, glast,
    send, recv, local,
):
    here = Place()
    net = Net(here, send, recv, local)
    net.greet(ALL_NEAR)
    gs = ShardSum(net, terms, GROWS, gheld, ggift, gpassed, gplus, gminus, glast)
    at = ShardSum(net, agrads, BLOCK, held, gift, passed, plus, minus, last)
    fz = RingGather(net, fblk, ffull)

    for shares in (gs, at):
        for dx in (2, 1, 3):
            for dy in (1, 0):
                shares.pair(dx, dy)
    gs.pass_on(1)
    gs.pass_on(0)
    at.pass_on(1)
    at.pass_on(0)
    for shares in (gs, at):
        shares.pair(0, 1)
        shares.pair(0, 0)
    fz.forward()

    def spread(zz, block):
        gate_o[:, span(zz, FFD)] = block[:, :FFD].astype(F32)
        up_o[:, span(zz, FFD)] = block[:, FFD : 2 * FFD].astype(F32)
        down_o[span(zz, FFD), :] = block[:, 2 * FFD :].astype(F32).T

    spread(here.z, fblk[...])
    for shares in (gs, at):
        shares.close(1)
        shares.close(0)
    gblk[...] = gs.result().astype(BF16)
    gz = RingGather(net, gblk, gfull)
    ablk[...] = at.result().astype(BF16)
    az = RingGather(net, ablk, afull)
    afull[az.at(0), :] = ablk[...]
    gfull[gz.at(0), :] = gblk[...]
    fz.left()
    spread(ring(here.z, 3), ffull[fz.at(3), :])
    fz.right()
    spread(ring(here.z, 1), ffull[fz.at(1), :])
    gz.forward()
    az.forward()
    fz.far()
    spread(ring(here.z, 2), ffull[fz.at(2), :])
    for shares in (gz, az):
        shares.left()
        shares.right()
        shares.far()
    blocks = [afull[i * BLOCK : (i + 1) * BLOCK, :].astype(F32) for i in range(4)]
    for i in range(4):
        query_o[:, i * HEAD : (i + 1) * HEAD] = blocks[i][:, :HEAD]
        wout_o[i * HEAD : (i + 1) * HEAD, :] = blocks[i][:, 3 * HEAD :].T
    for g in range(2):
        pair = blocks[2 * g][:, HEAD : 3 * HEAD] + blocks[2 * g + 1][:, HEAD : 3 * HEAD]
        key_o[:, g * HEAD : (g + 1) * HEAD] = pair[:, :HEAD]
        value_o[:, g * HEAD : (g + 1) * HEAD] = pair[:, HEAD:]
    gain = sum(gfull[i * GROWS : (i + 1) * GROWS, :].astype(F32) for i in range(4))
    gone_o[...] = gain[0:1]
    gtwo_o[...] = gain[1:2]
    net.drain()


def call_r(agrads, terms, fblk):
    return pl.pallas_call(
        kernel_r,
        out_shape=[
            out((1, 128), F32), out((BLOCK, 4 * HEAD), F32), out((BLOCK, 2 * HEAD), F32),
            out((BLOCK, 2 * HEAD), F32), out((4 * HEAD, BLOCK), F32), out((1, 128), F32),
            out((BLOCK, 4 * FFD), F32), out((BLOCK, 4 * FFD), F32), out((4 * FFD, BLOCK), F32),
        ],
        in_specs=[ANY, ANY, VM],
        out_specs=[VM] * 9,
        scratch_shapes=[
            pltpu.VMEM((4 * BLOCK, 3 * FFD), BF16), pltpu.VMEM((4 * BLOCK, 4 * HEAD), BF16),
            pltpu.VMEM((4 * GROWS, 128), BF16), pltpu.VMEM((BLOCK, 4 * HEAD), BF16),
            pltpu.VMEM((GROWS, 128), BF16),
            *shard_sum_scratch(BLOCK, 4 * HEAD), *shard_sum_scratch(GROWS, 128),
            *near_sems(80, 24),
        ],
        compiler_params=params(3),
        name="gather_grads",
    )(agrads, terms, fblk)


def tables(parent_row):
    index = jnp.arange(NSEG)
    links = (parent_row[:, None] == index[None, :]).astype(F32)
    reached = links + jnp.eye(NSEG, dtype=F32)
    for _ in range(4):
        reached = jnp.minimum(jnp.dot(reached, reached, precision=HIGHEST), 1.0)
    depth = jnp.sum(reached, 1) - 1.0
    token = jnp.arange(TREE)
    segment = token // SEG
    offset = token % SEG
    onehot = (segment[:, None] == index[None, :]).astype(F32)
    position = jnp.dot(onehot, depth, precision=HIGHEST) * SEG + offset.astype(F32)
    frequency = jnp.power(THETA, -(jnp.arange(HALF, dtype=F32) * 2.0) / HEAD)
    angles = position[:, None] * frequency[None, :]
    linked = nt(jnp.dot(onehot, reached, precision=HIGHEST), onehot) > 0.5
    allowed = linked & (
        (segment[:, None] != segment[None, :]) | (offset[None, :] <= offset[:, None])
    )
    return jnp.cos(angles), jnp.sin(angles), allowed.astype(BF16)


def local(
    tokens, parents, gain_attn, w_query, key_weight, value_weight, w_out, gain_ffn, w_gate, w_up,
    w_down, cotangent,
):
    z = lax.axis_index("ctx")

    def cols(w, at, size):
        return lax.dynamic_slice_in_dim(w, at, size, 1)

    def rows(w, at, size):
        return lax.dynamic_slice_in_dim(w, at, size, 0)

    gblk = jnp.pad(jnp.stack([gain_attn, gain_ffn], 0), ((0, GROWS - 2), (0, 0)))
    ablk = jnp.concatenate(
        [
            cols(w_query, z * HEAD, HEAD),
            cols(key_weight, (z // 2) * HEAD, HEAD),
            cols(value_weight, (z // 2) * HEAD, HEAD),
            rows(w_out, z * HEAD, HEAD).T,
        ],
        1,
    )
    fblk = jnp.concatenate(
        [cols(w_gate, z * FFD, FFD), cols(w_up, z * FFD, FFD), rows(w_down, z * FFD, FFD).T], 1
    )
    cosine, sine, allowed = tables(parents[0])
    n1, q, k, v, a, p, hidden, n2, aw, gains, fw, cf = call_a(
        tokens, cotangent, ablk, fblk, gblk, cosine, sine, allowed
    )
    dh, low, output, fgrads, term = call_f(n2, hidden, fw, cf, gains)
    d_tokens, agrads, terms, fsum = call_b(
        low, dh, tokens, cosine, sine, gains, term, p, q, k, v, a, n1, aw, fgrads
    )
    g_one, query, key, value, wout, g_two, gate, up, down = call_r(agrads, terms, fsum)
    return (
        output, d_tokens, g_one.reshape(128), query, key, value, wout, g_two.reshape(128), gate, up,
        down,
    )


def solution(mesh):
    rows = P(("shard", "ctx"), None)
    weight = P("shard", "tp")
    turned = P("tp", "shard")
    vector = P("shard")
    return jax.shard_map(
        local,
        mesh=mesh,
        in_specs=(
            rows, P("shard", None), vector, weight, weight, weight, turned, vector,
            weight, weight, turned, rows,
        ),
        out_specs=(
            rows, rows, vector, weight, weight, weight, turned, vector, weight, weight, turned,
        ),
        check_vma=False,
    )
```

time: 1060 us -> 368 us (0.35); the launches traced: 1050 us -> 367 us
  waiting for transfers between devices: 781 us -> 0 us
  Pallas kernels: 3.69 us -> 341 us
  matrix products: 85.7 us -> 4.01 us
  local copies, waits for them, and re-layouts: 91.2 us -> 15.8 us
  other arithmetic: 53.5 us -> 5.46 us
  between operations: 15.2 us -> 0.84 us
  starting transfers between devices: 11.1 us -> 0 us
    all_gather x9 -> x0, waiting for transfers between devices: 401 us -> none  [the longest x1 80.1 us: local(): ffn_w = lax.all_gather(ffn_mine, 'shard', axis=0, tiled=True)]
    pallas_call x0 -> x4, Pallas kernels: none -> 341 us  [the longest x1 100 us: call_a(): pl.pallas_call(kernel_a, out_shape=[out((TREE, WIDTH)), out((TREE, HEAD))...]
    reduce_scatter x4 -> x0, waiting for transfers between devices: 284 us -> none  [scatter(): lax.psum_scatter(part.astype(BF16), ('ctx', 'tp'), scatter_dimension=0, t...]
    unnamed x17 -> x0, waiting for transfers between devices: 95.6 us -> none
    dot_general x28 -> x2, matrix products: 83.8 us -> 2.16 us  [the longest x1 1.77 us: nt(): lax.dot_general(left, right, (((1,), (1,)), ((), ())), preferred_element_...]
    unnamed x133 -> x39, local copies, waits for them, and re-layouts: 55.1 us -> 12.1 us
    concatenate x5 -> x0, other arithmetic: 24.6 us -> none  [the longest x1 21.4 us: local(): jnp.concatenate([contract(n2, dg, 0, 0).astype(BF16), contract(n2, du, 0,...]
    slice x5 -> x0, local copies, waits for them, and re-layouts: 23.8 us -> none  [the longest x2 13 us: wide(): parts[i]]
  transfers between devices with their start and end apart: 15 -> 0, of which waited for: 15 -> 0; matrix products, arithmetic and copies ran while one was open for 12% -> 0% of each run, Pallas kernels for 0% -> 0%
where the time goes in v2:
time: 368 us; the launch traced here: 367 us
  Pallas kernels  341 us (93%)
  local copies, waits for them, and re-layouts  15.8 us (4%)
  other arithmetic  5.46 us (1%)
  matrix products  4.01 us (1%)
    pallas_call x1, Pallas kernels, call_a(): pl.pallas_call(kernel_a, out_shape=[out((TREE, WIDTH)), out((TREE, HEAD))...  100 us
    pallas_call x1, Pallas kernels, call_f(): pl.pallas_call(kernel_f, out_shape=[out((ROWS, WIDTH), F32), out((ROWS, W...  100 us
    pallas_call x1, Pallas kernels, call_b(): pl.pallas_call(kernel_b, out_shape=[out((ROWS, WIDTH)), out((WIDTH, 4 * H...  92.7 us
    pallas_call x1, Pallas kernels, call_r(): pl.pallas_call(kernel_r, out_shape=[out((1, 128), F32), out((BLOCK, 4 * H...  47.2 us
    unnamed x39, local copies, waits for them, and re-layouts  12.1 us

profile of v2, /device:TPU:1, one launch (start us, length us, event | category | flops | bytes accessed | tf_op | source)
XLA Modules:
  0.0 366.6 jit_solution(9954041315120364427)
XLA Ops:
  0.6 0.0 copy-start
  0.7 1.0 convolution_minimum_fusion.3
  1.7 0.1 convolution_minimum_fusion.2
  1.8 0.1 convolution_minimum_fusion.1
  2.0 0.2 fusion.22
  2.2 1.3 fusion.6.gblk
  3.4 0.4 convolution_reduce_fusion
  3.9 0.9 constant_dynamic-slice_fusion.6
  4.7 0.8 constant_dynamic-slice_fusion.3
  5.6 0.1 copy.25
  5.7 0.9 constant_dynamic-slice_fusion.4
  6.6 0.7 pad_maximum_fusion.1.ablk
  7.3 0.4 fusion
  7.7 0.0 copy-done
  7.7 0.1 copy.26
  7.9 1.1 constant_dynamic-slice_fusion.1
  9.0 0.9 pad_maximum_fusion.fblk
  9.9 2.5 multiply_sine_fusion
  12.4 1.8 and_convert_fusion.allowed
  14.2 100.3 %attend.1 = (bf16[768,2048]{1,0:T(8,128)(2,1)}, bf16[768,256]{1,0:T(8,128)(2,1)}, bf16[768,256]{1,0:T(8,128)(2,1)}, bf16[768,256]{1,0:T(8,128)(2,1)}, bf16[768,2...) custom-call(bf16[192,2048]{1,0:T(8,128)(2,1)} %tok.3, ...), custom_call_target="tpu_custom_call" | custom-call | tf_op jit(solution)/shard_map/attend/pallas_call | solution.py:521
  114.5 100.3 %feed.1 = (f32[192,2048]{1,0:T(8,128)}, bf16[192,2048]{1,0:T(8,128)(2,1)}, bf16[192,2048]{1,0:T(8,128)(2,1)}, bf16[2048,3072]{1,0:T(8,128)(2,1)}, f32[1,2048]{1,0:T(1,128)}) custom-call(bf16[192,2048]{1,0:T(8,128)(2,1)} %get-tuple-element.41.n2_in, f32[192,2048]{1,0:T(8,128)} %get-tuple-element.42.h_in, bf16[2048,3072]{1,0:T(8,128)(2,1)} %get-tuple-element.43.fw, ...), custom_call_target="tpu_custom_call" | custom-call | tf_op jit(solution)/shard_map/feed/pallas_call | solution.py:671
  214.8 92.7 %attend_back.1 = (bf16[192,2048]{1,0:T(8,128)(2,1)}, bf16[2048,1024]{1,0:T(8,128)(2,1)}, bf16[512,128]{1,0:T(8,128)(2,1)}, bf16[128,3072]{1,0:T(8,128)(2,1)}) custom-call(bf16[192,2048]{1,0:T(8,128)(2,1)} %get-tuple-element.47.low_in, f32[192,2048]{1,0:T(8,128)} %get-tuple-element.48.dh_in, bf16[192,2048]{1,0:T(8,128)(2,1)} %tok.3, ...), custom_call_target="tpu_custom_call" | custom-call | tf_op jit(solution)/shard_map/attend_back/pallas_call | solution.py:822
  307.5 0.0 copy-start.5
  307.6 0.0 copy-start.6
  307.6 47.2 %gather_grads.1 = (f32[1,128]{1,0:T(1,128)}, f32[128,1024]{1,0:T(8,128)}, f32[128,512]{1,0:T(8,128)}, f32[128,512]{1,0:T(8,128)}, f32[1024,128]{1,0:T(8,128)}, /...) custom-call(bf16[2048,1024]{1,0:T(8,128)(2,1)} %get-tuple-element.59.agrads, ...), custom_call_target="tpu_custom_call" | custom-call | tf_op jit(solution)/shard_map/gather_grads/pallas_call | solution.py:913
  354.7 0.0 copy-start.12
  354.8 0.0 copy-start.8
  354.8 0.0 copy-done.5
  354.8 0.0 copy-start.10
  354.8 0.0 copy-start.9
  354.8 0.9 copy.38
  355.7 0.0 copy-done.6
  355.7 0.0 copy-start.7
  355.7 0.0 copy-start.11
  355.7 0.0 copy-start.4
  355.7 0.9 copy.39
  356.6 0.0 copy-done.12
  356.6 0.5 copy.40
  357.1 0.0 copy-done.8
  357.1 0.8 copy.41
  357.9 0.0 copy-done.10
  357.9 0.7 copy.42
  358.6 0.0 copy-done.9
  358.6 0.7 copy.43
  359.3 0.0 copy-done.7
  359.3 0.8 copy.44
  360.1 0.0 copy-done.11
  360.1 0.5 copy.45
  360.6 0.0 copy-done.4
  360.6 0.0 copy-start.3
  360.6 1.3 copy.46
  361.9 1.0 copy-done.3
  363.0 0.0 copy-start.2
  363.0 0.0 copy-start.1
  363.0 1.3 copy.47
  364.3 1.0 copy-done.2
  365.3 1.3 copy.48
  366.6 0.0 copy-done.1
  (4 shorter events, 0.1 us)
Async XLA Ops:
  0.6 7.1 %copy-start = (bf16[4096,128]{1,0:T(8,128)(2,1)S(1)}, bf16[4096,128]{1,0:T(8,128)(2,1)}, u32[]{:S(2)}) copy-start(bf16[4096,128]{1,0:T(8,128)(2,1)} %param.22) | copy-start | bytes 3145732
  307.5 47.2 %copy-start.5 = (bf16[192,2048]{1,0:T(8,128)(2,1)S(1)}, bf16[192,2048]{1,0:T(8,128)(2,1)}, u32[]{:S(2)}) copy-start(bf16[192,2048]{1,0:T(8,128)(2,1)} %get-tuple-element.92) | copy-start | bytes 2359300
  307.6 48.1 %copy-start.6 = (bf16[192,2048]{1,0:T(8,128)(2,1)S(1)}, bf16[192,2048]{1,0:T(8,128)(2,1)}, u32[]{:S(2)}) copy-start(bf16[192,2048]{1,0:T(8,128)(2,1)} %get-tuple-element.93) | copy-start | bytes 2359300
  354.7 1.8 copy-start.12
  354.8 2.3 copy-start.8
  354.8 3.1 copy-start.10
  354.8 3.8 %copy-start.9 = (f32[128,512]{1,0:T(8,128)S(1)}, f32[128,512]{1,0:T(8,128)}, u32[]{:S(2)}) copy-start(f32[128,512]{1,0:T(8,128)} %get-tuple-element.97) | copy-start | bytes 786436
  355.7 3.6 copy-start.7
  355.7 4.4 %copy-start.11 = (f32[1,128]{1,0:T(1,128)S(1)}, f32[1,128]{1,0:T(1,128)}, u32[]{:S(2)}) copy-start(f32[1,128]{1,0:T(1,128)} %get-tuple-element.67) | copy-start | bytes 1540
  355.7 4.9 %copy-start.4 = (f32[128,4096]{1,0:T(8,128)S(1)}, f32[128,4096]{1,0:T(8,128)}, u32[]{:S(2)}) copy-start(f32[128,4096]{1,0:T(8,128)} %get-tuple-element.100) | copy-start | bytes 6291460
  360.6 2.3 copy-start.3
  363.0 2.3 copy-start.2
  363.0 3.7 %copy-start.1 = (bf16[4096,128]{1,0:T(8,128)(2,1)S(1)}, bf16[4096,128]{1,0:T(8,128)(2,1)}, u32[]{:S(2)}) copy-start(bf16[4096,128]{1,0:T(8,128)(2,1)} %param.22) | copy-start | bytes 3145732
